TPU v7x, 256 devices: a whole 4x4x8 slice. The times are simulated.
256 devices in a mesh: row: 8 (over z_hi, x), col: 16 (over z_lo, y), chan: 2 (over core).
Axes of the slice: x: 4, y: 4, z: 8 (z_hi: 2, z_lo: 4; z = z_hi * 4 + z_lo), core: 2. Of those that a mesh axis runs over, the one named last changes fastest.
Arguments:
- image: bfloat16 [192, 512, 2048], P('chan', 'row', 'col'), may hold values from -6 to 6
- kernel_one: float32 [192, 7, 7], P('chan'), may hold values from -0.875 to 0.875
- kbias_one: float32 [192], P('chan'), may hold values from -3 to 3
- gain_one: float32 [192], replicated, may hold values from 0.1 to 1.9
- shift_one: float32 [192], replicated, may hold values from -3 to 3
- expand_one: bfloat16 [192, 768], P(None, 'chan'), may hold values from -0.4375 to 0.4375
- ebias_one: float32 [768], P('chan'), may hold values from -3 to 3
- reduce_one: bfloat16 [768, 192], P('chan'), may hold values from -0.21875 to 0.21875
- rbias_one: float32 [192], replicated, may hold values from -3 to 3
- scale_one: float32 [192], replicated, may hold values from 0.3 to 1
- pool_gain: float32 [192], replicated, may hold values from 0.1 to 1.9
- pool_shift: float32 [192], replicated, may hold values from -3 to 3
- pool_weight: bfloat16 [4, 192, 384], P(None, None, 'chan'), may hold values from -0.21875 to 0.21875
- pool_bias: float32 [384], P('chan'), may hold values from -3 to 3
- kernel_two: float32 [384, 7, 7], P('chan'), may hold values from -0.875 to 0.875
- kbias_two: float32 [384], P('chan'), may hold values from -3 to 3
- gain_two: float32 [384], replicated, may hold values from 0.1 to 1.9
- shift_two: float32 [384], replicated, may hold values from -3 to 3
- expand_two: bfloat16 [384, 1536], P(None, 'chan'), may hold values from -0.3125 to 0.3125
- ebias_two: float32 [1536], P('chan'), may hold values from -3 to 3
- reduce_two: bfloat16 [1536, 384], P('chan'), may hold values from -0.15625 to 0.15625
- rbias_two: float32 [384], replicated, may hold values from -3 to 3
- scale_two: float32 [384], replicated, may hold values from 0.3 to 1
Outputs:
- block_one: bfloat16 [192, 512, 2048], P('chan', 'row', 'col')
- block_two: bfloat16 [384, 256, 1024], P('chan', 'row', 'col')
All inputs are finite; a program needn't handle non-finite values.
Results may differ from a plain program's by a relative error of at most 0.017.
Values may be sent and summed in bfloat16 or wider, within the bound.
No kernel may reach another device: no remote copies, remote signals or barrier semaphores. Data moves between devices by JAX's collectives and lax.ppermute only.
A program may use at most 128 MiB of HBM per device.

v0:
```python
import jax
import jax.numpy as jnp
from jax import lax
from jax.sharding import PartitionSpec as P


def with_halo(x, sides, width):
    for axis, dim in sides:
        size, length = (lax.axis_size(axis), x.shape[dim])
        up = [(i, (i + 1) % size) for i in range(size - 1)]
        down = [(j, i) for i, j in up]
        last = lax.slice_in_dim(x, length - width, length, axis=dim)
        initial = lax.slice_in_dim(x, 0, width, axis=dim)
        before = lax.ppermute(last, axis, up)
        after = lax.ppermute(initial, axis, down)
        x = jnp.concatenate([before, x, after], axis=dim)
    return x


def depthwise(padded, kernel, kbias, rows, cols):
    total = jnp.zeros((padded.shape[0], rows, cols), jnp.float32)
    for first in range(7):
        for second in range(7):
            window = padded[:, first : first + rows, second : second + cols].astype(jnp.float32)
            total = total + window * kernel[:, first, second][:, None, None]
    return total + kbias[:, None, None]


def channel_norm(values, gain, shift):
    center = values - jnp.mean(values, axis=0, keepdims=True)
    spread = jnp.mean(center * center, axis=0, keepdims=True)
    return center * lax.rsqrt(spread + 1e-06) * gain[:, None, None] + shift[:, None, None]


def expanded(full, gain, shift, expand, ebias):
    normed = channel_norm(full.astype(jnp.float32), gain, shift).astype(jnp.bfloat16)
    flat = normed.reshape(full.shape[0], -1)
    inner = jnp.einsum("cp,cf->fp", flat, expand, preferred_element_type=jnp.float32)
    return jax.nn.gelu(inner + ebias[:, None], approximate=False).astype(jnp.bfloat16)


def pool_block(whole_block, pool_gain, pool_shift, weight, bias):
    full_width, rows, cols = whole_block.shape
    pnorm = channel_norm(whole_block.astype(jnp.float32), pool_gain, pool_shift).astype(
        jnp.bfloat16
    )
    half_rows, half_cols = (rows // 2, cols // 2)
    quads = pnorm.reshape(full_width, half_rows, 2, half_cols, 2)
    total = jnp.zeros((weight.shape[2], half_rows * half_cols), jnp.float32)
    for down in range(2):
        for right in range(2):
            sub = quads[:, :, down, :, right].reshape(full_width, -1)
            total = total + jnp.einsum(
                "cp,co->op", sub, weight[2 * down + right], preferred_element_type=jnp.float32
            )
    return (
        (total + bias[:, None]).astype(jnp.bfloat16).reshape(weight.shape[2], half_rows, half_cols)
    )


def on_device(
    image,
    kernel_one,
    kbias_one,
    gain_one,
    shift_one,
    expand_one,
    ebias_one,
    reduce_one,
    rbias_one,
    scale_one,
    pool_gain,
    pool_shift,
    pool_weight,
    pool_bias,
    kernel_two,
    kbias_two,
    gain_two,
    shift_two,
    expand_two,
    ebias_two,
    reduce_two,
    rbias_two,
    scale_two,
):
    chan_index = lax.axis_index("chan")
    local_width, rows, cols = image.shape
    pixels = rows * cols
    half_rows, half_cols = (rows // 2, cols // 2)
    coarse_local = pool_weight.shape[2]
    padded = with_halo(image, (("row", 1), ("col", 2)), 3)
    mixed_one = depthwise(padded, kernel_one, kbias_one, rows, cols).astype(jnp.bfloat16)
    full_one = lax.all_gather(mixed_one, "chan", axis=0, tiled=True)
    hidden_one = expanded(full_one, gain_one, shift_one, expand_one, ebias_one)
    columns = reduce_one
    summed = lax.psum_scatter(
        jnp.einsum("fc,fp->cp", columns, hidden_one, preferred_element_type=jnp.float32).astype(
            jnp.bfloat16
        ),
        "chan",
        scatter_dimension=0,
        tiled=True,
    ).astype(jnp.float32)
    rb_local = lax.dynamic_slice_in_dim(rbias_one, chan_index * local_width, local_width, 0)
    sc_local = lax.dynamic_slice_in_dim(scale_one, chan_index * local_width, local_width, 0)
    result = image.reshape(local_width, pixels).astype(jnp.float32) + sc_local[:, None] * (
        summed + rb_local[:, None]
    )
    block_one = result.astype(jnp.bfloat16).reshape(local_width, rows, cols)
    whole_block = lax.all_gather(block_one, "chan", axis=0, tiled=True)
    pooled = pool_block(whole_block, pool_gain, pool_shift, pool_weight, pool_bias)
    col_count = lax.axis_size("col")
    group = coarse_local // col_count
    parts = pooled.reshape(col_count, group, half_rows, half_cols)
    moved = lax.all_to_all(parts, "col", split_axis=0, concat_axis=3, tiled=True)[0]
    rimmed = with_halo(moved, (("row", 1),), 3)
    rimmed = jnp.pad(rimmed, ((0, 0), (0, 0), (3, 3)))
    col_index = lax.axis_index("col")
    kernel_part = lax.dynamic_slice_in_dim(kernel_two, col_index * group, group, 0)
    kbias_part = lax.dynamic_slice_in_dim(kbias_two, col_index * group, group, 0)
    strip = depthwise(rimmed, kernel_part, kbias_part, half_rows, moved.shape[2]).astype(
        jnp.bfloat16
    )
    mixed_two = lax.all_to_all(strip, "col", split_axis=2, concat_axis=0, tiled=True)
    full_two = lax.all_gather(mixed_two, "chan", axis=0, tiled=True)
    hidden_two = expanded(full_two, gain_two, shift_two, expand_two, ebias_two)
    columns = reduce_two
    summed_two = lax.psum_scatter(
        jnp.einsum("fc,fp->cp", columns, hidden_two, preferred_element_type=jnp.float32).astype(
            jnp.bfloat16
        ),
        "chan",
        scatter_dimension=0,
        tiled=True,
    ).astype(jnp.float32)
    rb_two = lax.dynamic_slice_in_dim(rbias_two, chan_index * coarse_local, coarse_local, 0)
    sc_two = lax.dynamic_slice_in_dim(scale_two, chan_index * coarse_local, coarse_local, 0)
    result_two = pooled.reshape(coarse_local, -1).astype(jnp.float32) + sc_two[:, None] * (
        summed_two + rb_two[:, None]
    )
    block_two = result_two.astype(jnp.bfloat16).reshape(coarse_local, half_rows, half_cols)
    return (block_one, block_two)


def solution(mesh):
    return jax.shard_map(
        on_device,
        mesh=mesh,
        in_specs=(
            P("chan", "row", "col"),
            P("chan", None, None),
            P("chan"),
            P(),
            P(),
            P(None, "chan"),
            P("chan"),
            P("chan", None),
            P(),
            P(),
            P(),
            P(),
            P(None, None, "chan"),
            P("chan"),
            P("chan", None, None),
            P("chan"),
            P(),
            P(),
            P(None, "chan"),
            P("chan"),
            P("chan", None),
            P(),
            P(),
        ),
        out_specs=(P("chan", "row", "col"), P("chan", "row", "col")),
        check_vma=False,
    )
```

profile of v0, /device:TPU:1, one launch (start us, length us, event | category | flops | bytes accessed | tf_op | source)
XLA Modules:
  0.0 415.1 jit_solution(13028059309873289836)
XLA Ops:
  7.2 3.7 copy.33
  11.0 4.0 collective-permute-start
  15.0 1.3 collective-permute-start.1
  17.1 3.6 collective-permute-done.1
  20.8 3.2 collective-permute-start.2
  24.0 1.3 collective-permute-start.3
  25.3 3.6 collective-permute-done.3
  28.9 4.2 %maximum_maximum_fusion = (bf16[96,70,131]{0,1,2:T(8,128)(2,1)S(1)}, bf16[96,70,131]{0,1,2:T(8,128)(2,1)S(1)}) fusion(bf16[96,3,128]{0,1,2:T(4,128)(2,1)S(1)} %collective-permute-done.1, bf16[96,64,128]{0,1,2:T(8,128)(2,1)S(1)} %copy.33, bf16[96,3,128]{0,1,2:T(4,128)(2,1)S(1)} %collective-permute-done, bf16[96,70,3]{0,1,2:T(8,128)(2,1)S(1)} %collective-permute-done.2, ...), kind=kLoop, calls=%fused_computation.92 | loop fusion | flops 14085120 | bytes 5322240 | tf_op jit(solution)/shard_map/concatenate | solution.py:16
  33.1 33.2 %add_convert_fusion = bf16[96,64,128]{0,1,2:T(8,128)(2,1)} fusion(bf16[96,64,128]{0,1,2:T(8,128)(2,1)S(1)} %copy.33, bf16[96,3,128]{0,1,2:T(4,128)(2,1)S(1)} %collective-permute-done.1, bf16[96,3,128]{0,1,2:T(4,128)(2,1)S(1)} %collective-permute-done, bf16[96,70,131]{0,1,2:T(8,128)(2,1)S(1)} %get-tuple-element.9, ...), kind=kLoop, calls=%fused_computation.66 | loop fusion | flops 130547712 | bytes 69372672 | tf_op jit(solution)/shard_map/convert_element_type | solution.py:92
  66.3 4.4 %copy.40 = bf16[96,64,128]{2,1,0:T(8,128)(2,1)} copy(bf16[96,64,128]{0,1,2:T(8,128)(2,1)} %add_convert_fusion) | data formatting | bytes 3145728 | tf_op jit(solution)/shard_map/convert_element_type | solution.py:92
  70.7 33.1 %all-gather.4.cloned.1.call-done = bf16[192,64,128]{2,1,0:T(8,128)(2,1)} async-done(((bf16[96,64,128]{2,1,0:T(8,128)(2,1)}), bf16[192,64,128]{2,1,0:T(8,128)(2,1)}) %all-gather.4.cloned.1.call-update) | async-done | bytes 3145744 | tf_op jit(solution)/shard_map/all_gather | solution.py:93
  103.9 2.6 convert_reduce_fusion.1
  107.6 2.7 fusion.30
  110.4 42.0 %fusion.18 = bf16[192,8192]{1,0:T(8,128)(2,1)} fusion(bf16[384,192]{0,1:T(8,128)(2,1)S(1)} %copy-done.16, bf16[192,384]{1,0:T(8,128)(2,1)S(1)} %copy-done.17, f32[384]{0:T(512)S(1)} %copy-done.19, bf16[24,8,64,128]{3,2,1,0:T(8,128)(2,1)} %bitcast.403), kind=kOutput, calls=%fused_computation.25 | convolution fusion | flops 2625110016 | bytes 6587904 | tf_op jit(solution)/shard_map/fc,fp->cp/dot_general | solution.py:97
  152.5 3.5 copy.34
  156.2 13.8 %reduce-scatter.3.cloned.1.call-done = bf16[96,8192]{1,0:T(8,128)(2,1)} async-done(((bf16[192,8192]{1,0:T(8,128)(2,1)}), bf16[96,8192]{1,0:T(8,128)(2,1)}) %reduce-scatter.3.cloned.1.call-update) | async-done | bytes 1572880 | tf_op jit(solution)/shard_map/reduce_scatter | solution.py:96
  170.0 5.2 %fusion.69 = bf16[12,8,64,128]{3,1,2,0:T(8,128)(2,1)S(1)} fusion(bf16[96,8192]{1,0:T(8,128)(2,1)} %reduce-scatter.3.cloned.1.call-done, f32[12,8,64,128]{3,2,1,0:T(8,128)} %bitcast.394, f32[96]{0:T(128)S(1)} %dynamic_slice.19, f32[96]{0:T(128)S(1)} %dynamic_slice.18), kind=kLoop, calls=%fused_computation.106 | loop fusion | flops 3932160 | bytes 6292224
  175.1 1.6 copy.55
  176.7 19.1 %all-gather.6.cloned.1.call-done = bf16[192,64,128]{2,1,0:T(8,128)(2,1)} async-done(((bf16[96,64,128]{2,1,0:T(8,128)(2,1)}), bf16[192,64,128]{2,1,0:T(8,128)(2,1)}) %all-gather.6.cloned.1.call-update) | async-done | bytes 3145744 | tf_op jit(solution)/shard_map/all_gather | solution.py:110
  195.8 2.6 convert_reduce_fusion
  199.6 2.7 fusion.26
  202.2 6.8 %copy.41 = bf16[192,64,128]{0,2,1:T(8,128)(2,1)} copy(bf16[192,64,128]{2,1,0:T(8,128)(2,1)} %fusion.26) | data formatting | bytes 6291456 | tf_op jit(solution)/shard_map/convert_element_type | solution.py:44
  209.1 7.5 %reshape.76 = bf16[192,32,2,64,2]{0,4,3,2,1:T(2,128)(2,1)} reshape(bf16[192,64,128]{0,2,1:T(8,128)(2,1)} %copy.41) | data formatting | bytes 6291456 | tf_op jit(solution)/shard_map/reshape | solution.py:48
  216.6 10.5 %fusion.159 = (bf16[192,32,1,64,1]{0,4,3,2,1:T(2,128)(2,1)S(1)}, bf16[192,32,1,64,1]{0,4,3,2,1:T(2,128)(2,1)S(1)}, bf16[192,32,1,64,1]{0,4,3,2,1:T(2,128)(2,1)S(1)}, bf16[192,32,1,64,1]{0,4,3,2,1:T(2,128)(2,1)S(1)}) fusion(bf16[192,32,2,64,2]{0,4,3,2,1:T(2,128)(2,1)} %reshape.76), kind=kLoop, calls=%fused_computation.312 | loop fusion | bytes 6291456 | tf_op jit(solution)/shard_map/slice | solution.py:52
  230.5 1.9 reshape_reshape.3
  232.4 1.9 reshape.80
  234.2 6.9 %all-to-all-start = ((bf16[16,2,12288]{2,1,0:T(2,128)(2,1)}), bf16[16,2,12288]{2,1,0:T(2,128)(2,1)}, u32[]{:S(2)}, u32[]{:S(2)}) async-start(bf16[16,2,12288]{2,1,0:T(2,128)(2,1)} %reshape.80), calls=%async_computation.1 | async-start | bytes 1572864 | tf_op jit(solution)/shard_map/all_to_all | solution.py:115
  241.3 1.5 fusion.87
  242.8 16.9 %all-to-all-done = bf16[16,2,12288]{2,1,0:T(2,128)(2,1)} async-done(((bf16[16,2,12288]{2,1,0:T(2,128)(2,1)}), bf16[16,2,12288]{2,1,0:T(2,128)(2,1)}, u32[]{:S(2)}, u32[]{:S(2)}) %all-to-all-start) | async-done | bytes 786464 | tf_op jit(solution)/shard_map/all_to_all | solution.py:115
  259.7 3.0 reshape.81
  262.7 2.2 copy.42
  264.9 2.7 squeeze.19
  267.7 1.3 collective-permute-start.5
  269.0 4.0 collective-permute-start.4
  273.1 1.5 collective-permute-done.4
  275.7 15.3 %add_convert_fusion.2 = bf16[12,32,1024]{2,1,0:T(8,128)(2,1)S(1)} fusion(bf16[12,32,1024]{2,1,0:T(8,128)(2,1)S(1)} %squeeze.19, bf16[12,3,1024]{2,1,0:T(4,128)(2,1)S(1)} %collective-permute-done.4, bf16[12,38,1030]{2,1,0:T(8,128)(2,1)S(1)} %fusion.74, bf16[12,35,1024]{2,1,0:T(8,128)(2,1)S(1)} %constant_dynamic-update-slice_fusion, f32[12]{0:T(128)S(1)} %dynamic_slice.22, ...), kind=kLoop, calls=%fused_computation.108 | loop fusion | flops 61734912 | bytes 37038432 | tf_op jit(solution)/shard_map/convert_element_type | solution.py:121
  291.0 4.7 %copy.43 = bf16[12,32,1024]{1,0,2:T(8,128)(2,1)} copy(bf16[12,32,1024]{2,1,0:T(8,128)(2,1)S(1)} %add_convert_fusion.2) | data formatting | bytes 1572864 | tf_op jit(solution)/shard_map/convert_element_type | solution.py:121
  295.7 5.0 %reshape.82 = bf16[16,2,12288]{2,1,0:T(2,128)(2,1)S(1)} reshape(bf16[1024,12,32]{2,1,0:T(8,128)(2,1)} %bitcast.392) | data formatting | bytes 1572864
  300.7 25.4 %all_to_all.33 = bf16[16,2,12288]{2,1,0:T(2,128)(2,1)S(1)} all-to-all(bf16[16,2,12288]{2,1,0:T(2,128)(2,1)S(1)} %reshape.82), channel_id=1, replica_groups=mesh['row'=8,'col'=16,'chan'=2] {'col'}, dimensions={0} | all-to-all | bytes 1572864 | tf_op jit(solution)/shard_map/all_to_all | solution.py:124
  326.1 4.1 reshape.83
  330.2 5.2 %copy.44 = bf16[12,32,16,64]{3,1,0,2:T(8,128)(2,1)} copy(bf16[12,32,16,64]{1,0,3,2:T(8,128)(2,1)} %bitcast.393) | data formatting | bytes 1572864 | tf_op jit(solution)/shard_map/all_to_all | solution.py:124
  335.5 27.3 %all-gather.8.cloned.1.call-done = bf16[384,32,64]{2,1,0:T(8,128)(2,1)} async-done(((bf16[192,32,64]{2,1,0:T(8,128)(2,1)}), bf16[384,32,64]{2,1,0:T(8,128)(2,1)}) %all-gather.8.cloned.1.call-update) | async-done | bytes 1572880 | tf_op jit(solution)/shard_map/all_gather | solution.py:125
  362.8 4.8 %copy.45 = bf16[384,32,64]{0,2,1:T(8,128)(2,1)S(1)} copy(bf16[384,32,64]{2,1,0:T(8,128)(2,1)} %all-gather.8.cloned.1.call-done) | data formatting | bytes 3145728 | tf_op jit(solution)/shard_map/all_gather | solution.py:125
  369.2 1.7 fusion.54
  370.9 18.5 %fusion.58 = bf16[384,2048]{1,0:T(8,128)(2,1)} fusion(bf16[768,384]{1,0:T(8,128)(2,1)S(1)} %copy-done, bf16[384,2048]{0,1:T(8,128)(2,1)} %bitcast.404, bf16[384,768]{1,0:T(8,128)(2,1)S(1)} %copy-done.15, f32[768]{0:T(1024)S(1)} %copy-done.18), kind=kOutput, calls=%fused_computation.86 | convolution fusion | flops 2520514560 | bytes 4328448 | tf_op jit(solution)/shard_map/fc,fp->cp/dot_general | solution.py:129
  389.7 15.6 %reduce-scatter.5.cloned.1.call-done = bf16[192,2048]{1,0:T(8,128)(2,1)} async-done(((bf16[384,2048]{1,0:T(8,128)(2,1)}), bf16[192,2048]{1,0:T(8,128)(2,1)}) %reduce-scatter.5.cloned.1.call-update) | async-done | bytes 786448 | tf_op jit(solution)/shard_map/reduce_scatter | solution.py:128
  405.3 1.6 add_convert_fusion.1
  406.9 1.3 copy.47
  (91 shorter events, 10.0 us)
Async XLA Ops:
  7.2 363.8 %copy-start = (bf16[768,384]{1,0:T(8,128)(2,1)S(1)}, bf16[768,384]{1,0:T(8,128)(2,1)}, u32[]{:S(2)}) copy-start(bf16[768,384]{1,0:T(8,128)(2,1)} %param.43) | copy-start | bytes 1769476
  7.2 9.1 %copy-start.4 = (f32[96,7,7]{0,2,1:T(8,128)S(1)}, f32[96,7,7]{0,2,1:T(8,128)}, u32[]{:S(2)}) copy-start(f32[96,7,7]{0,2,1:T(8,128)} %param.24) | copy-start | bytes 56452
  7.2 96.7 %all-gather.4.cloned.1.call-start = ((), (), s32[]{:S(2)}) async-start(), calls=%async_computation.4 | async-start | bytes 4718592 | tf_op jit(solution)/shard_map/all_gather | solution.py:93
  11.0 6.1 %collective-permute-start = (bf16[96,3,128]{0,1,2:T(4,128)(2,1)S(1)}, bf16[96,3,128]{0,1,2:T(4,128)(2,1)S(1)}, u32[]{:S(2)}, u32[]{:S(2)}) collective-permute-start(bf16[96,3,128]{0,1,2:T(4,128)(2,1)S(1)} %get-tuple-element.12), channel_id=1, source_target_pairs={{0,32},{32,64},{64,96},{96,128},{128,160},{160,192},{192,224},{1,3... | collective-permute-start | bytes 221192 | tf_op jit(solution)/shard_map/ppermute | solution.py:14
  15.0 5.7 %collective-permute-start.1 = (bf16[96,3,128]{0,1,2:T(4,128)(2,1)S(1)}, bf16[96,3,128]{0,1,2:T(4,128)(2,1)S(1)}, u32[]{:S(2)}, u32[]{:S(2)}) collective-permute-start(bf16[96,3,128]{0,1,2:T(4,128)(2,1)S(1)} %get-tuple-element.13), channel_id=1, source_target_pairs={{32,0},{64,32},{96,64},{128,96},{160,128},{192,160},{224,192},{33,... | collective-permute-start | bytes 221192 | tf_op jit(solution)/shard_map/ppermute | solution.py:15
  20.7 12.4 %copy-start.14 = (f32[96]{0:T(128)S(1)}, f32[96]{0:T(128)}, u32[]{:S(2)}) copy-start(f32[96]{0:T(128)} %param.25) | copy-start | bytes 1156
  20.8 4.5 %collective-permute-start.2 = (bf16[96,70,3]{0,1,2:T(8,128)(2,1)S(1)}, bf16[96,70,3]{0,1,2:T(8,128)(2,1)S(1)}, u32[]{:S(2)}, u32[]{:S(2)}) collective-permute-start(bf16[96,70,3]{0,1,2:T(8,128)(2,1)S(1)} %get-tuple-element.10), channel_id=1, source_target_pairs={{0,2},{2,4},{4,6},{6,8},{8,10},{10,12},{12,14},{14,16},{16,18},{18... | collective-permute-start | bytes 120968 | tf_op jit(solution)/shard_map/ppermute | solution.py:14
  24.0 4.9 %collective-permute-start.3 = (bf16[96,70,3]{0,1,2:T(8,128)(2,1)S(1)}, bf16[96,70,3]{0,1,2:T(8,128)(2,1)S(1)}, u32[]{:S(2)}, u32[]{:S(2)}) collective-permute-start(bf16[96,70,3]{0,1,2:T(8,128)(2,1)S(1)} %get-tuple-element.11), channel_id=1, source_target_pairs={{2,0},{4,2},{6,4},{8,6},{10,8},{12,10},{14,12},{16,14},{18,16},{20... | collective-permute-start | bytes 120968 | tf_op jit(solution)/shard_map/ppermute | solution.py:15
  70.7 37.0 %copy-start.8 = (f32[192]{0:T(256)S(1)}, f32[192]{0:T(256)}, u32[]{:S(2)}) copy-start(f32[192]{0:T(256)} %param.27) | copy-start | bytes 2308
  70.7 37.0 %copy-start.9 = (f32[192]{0:T(256)S(1)}, f32[192]{0:T(256)}, u32[]{:S(2)}) copy-start(f32[192]{0:T(256)} %param.26) | copy-start | bytes 2308
  70.7 99.3 %reduce-scatter.3.cloned.1.call-start = ((), (), s32[]{:S(2)}) async-start(), calls=%async_computation.5 | async-start | bytes 4718592 | tf_op jit(solution)/shard_map/reduce_scatter | solution.py:96
  103.9 2.8 copy-start.1
  106.7 3.7 copy-start.16
  106.7 3.7 copy-start.17
  106.7 3.7 copy-start.19
  152.4 3.6 copy-start.20
  152.4 3.6 copy-start.21
  152.5 43.3 %all-gather.6.cloned.1.call-start = ((), (), s32[]{:S(2)}) async-start(), calls=%async_computation.6 | async-start | bytes 4718592 | tf_op jit(solution)/shard_map/all_gather | solution.py:110
  176.7 22.9 %copy-start.10 = (f32[192]{0:T(256)S(1)}, f32[192]{0:T(256)}, u32[]{:S(2)}) copy-start(f32[192]{0:T(256)} %param.34) | copy-start | bytes 2308
  176.7 22.9 %copy-start.11 = (f32[192]{0:T(256)S(1)}, f32[192]{0:T(256)}, u32[]{:S(2)}) copy-start(f32[192]{0:T(256)} %param.33) | copy-start | bytes 2308
  195.8 2.8 copy-start.2
  227.4 1.0 copy-start.3
  228.9 1.1 copy-start.7
  230.0 11.2 %copy-start.22 = (f32[192]{0:T(256)S(1)}, f32[192]{0:T(256)}, u32[]{:S(2)}) copy-start(f32[192]{0:T(256)} %param.38) | copy-start | bytes 2308
  234.2 25.4 %all-to-all-start = ((bf16[16,2,12288]{2,1,0:T(2,128)(2,1)}), bf16[16,2,12288]{2,1,0:T(2,128)(2,1)}, u32[]{:S(2)}, u32[]{:S(2)}) async-start(bf16[16,2,12288]{2,1,0:T(2,128)(2,1)} %reshape.80), calls=%async_computation.1 | async-start | bytes 1572864 | tf_op jit(solution)/shard_map/all_to_all | solution.py:115
  241.1 121.7 %all-gather.8.cloned.1.call-start = ((), (), s32[]{:S(2)}) async-start(), calls=%async_computation.7 | async-start | bytes 4718592 | tf_op jit(solution)/shard_map/all_gather | solution.py:125
  267.7 5.4 %collective-permute-start.5 = (bf16[12,3,1024]{2,1,0:T(4,128)(2,1)S(1)}, bf16[12,3,1024]{2,1,0:T(4,128)(2,1)S(1)}, u32[]{:S(2)}, u32[]{:S(2)}) collective-permute-start(bf16[12,3,1024]{2,1,0:T(4,128)(2,1)S(1)} %get-tuple-element.14), channel_id=1, source_target_pairs={{32,0},{64,32},{96,64},{128,96},{160,128},{192,160},{224,192},{33,... | collective-permute-start | bytes 221192 | tf_op jit(solution)/shard_map/ppermute | solution.py:15
  269.0 5.6 %collective-permute-start.4 = (bf16[12,3,1024]{2,1,0:T(4,128)(2,1)S(1)}, bf16[12,3,1024]{2,1,0:T(4,128)(2,1)S(1)}, u32[]{:S(2)}, u32[]{:S(2)}) collective-permute-start(bf16[12,3,1024]{2,1,0:T(4,128)(2,1)S(1)} %get-tuple-element.15), channel_id=1, source_target_pairs={{0,32},{32,64},{64,96},{96,128},{128,160},{160,192},{192,224},{1,3... | collective-permute-start | bytes 221192 | tf_op jit(solution)/shard_map/ppermute | solution.py:14
  335.5 33.7 %copy-start.5 = (f32[384]{0:T(512)S(1)}, f32[384]{0:T(512)}, u32[]{:S(2)}) copy-start(f32[384]{0:T(512)} %param.40) | copy-start | bytes 4612
  335.5 33.7 %copy-start.6 = (f32[384]{0:T(512)S(1)}, f32[384]{0:T(512)}, u32[]{:S(2)}) copy-start(f32[384]{0:T(512)} %param.39) | copy-start | bytes 4612
  335.5 69.8 %reduce-scatter.5.cloned.1.call-start = ((), (), s32[]{:S(2)}) async-start(), calls=%async_computation.8 | async-start | bytes 2359296 | tf_op jit(solution)/shard_map/reduce_scatter | solution.py:128
  367.7 3.3 copy-start.15
  367.7 3.2 copy-start.18
  370.9 18.6 %copy-start.12 = (f32[384]{0:T(512)S(1)}, f32[384]{0:T(512)}, u32[]{:S(2)}) copy-start(f32[384]{0:T(512)} %param.45) | copy-start | bytes 4612
  370.9 18.6 %copy-start.13 = (f32[384]{0:T(512)S(1)}, f32[384]{0:T(512)}, u32[]{:S(2)}) copy-start(f32[384]{0:T(512)} %param.44) | copy-start | bytes 4612
Sparse Core Ops, SparseCore 0:
  70.8 33.0 all-gather.3
  152.6 17.2 reduce-scatter.2
  176.8 18.9 all-gather.5
  335.6 27.2 all-gather.7
  389.6 15.6 reduce-scatter.4
where the time goes:
time: 423 us; the launch traced here: 415 us
  waiting for transfers between devices  135 us (32%)
  local copies, waits for them, and re-layouts  78.6 us (19%)
  other arithmetic  76.2 us (18%)
  matrix products  62.6 us (15%)
  blocking collectives  25.4 us (6%)
  starting transfers between devices  22.1 us (5%)
  between operations  14.8 us (3%)
    dot_general x1, matrix products, on_device(): jnp.einsum('fc,fp->cp', columns, hidden_one, preferred_element_type=jnp.f...  42 us
    convert_element_type x1, other arithmetic, on_device(): depthwise(padded, kernel_one, kbias_one, rows, cols).astype(jnp.bfloat16)  33.2 us
    all_gather x1, waiting for transfers between devices, on_device(): full_one = lax.all_gather(mixed_one, 'chan', axis=0, tiled=True)  33.1 us
    all_gather x1, waiting for transfers between devices, on_device(): full_two = lax.all_gather(mixed_two, 'chan', axis=0, tiled=True)  27.3 us
    all_to_all x1, blocking collectives, on_device(): lax.all_to_all(strip, 'col', split_axis=2, concat_axis=0, tiled=True)  25.4 us
    unnamed x57, local copies, waits for them, and re-layouts  21 us
    all_gather x1, waiting for transfers between devices, on_device(): whole_block = lax.all_gather(block_one, 'chan', axis=0, tiled=True)  19.1 us
    dot_general x1, matrix products, on_device(): jnp.einsum('fc,fp->cp', columns, hidden_two, preferred_element_type=jnp.f...  18.5 us
  transfers between devices with their start and end apart: 12, of which 10 were waited for; matrix products, arithmetic and copies ran while one was open for 1% of the time, Pallas kernels for 0%

commit v1 on v0

v1 whole, which is shorter than its diff:
```python
import functools

import jax
import jax.numpy as jnp
from jax import lax
from jax.experimental import pallas as pl
from jax.experimental.pallas import tpu as pltpu
from jax.sharding import PartitionSpec as P

F32 = jnp.float32
BF16 = jnp.bfloat16
LANES = 128
SIDE = 3
TAPS = 7
VMEM_LIMIT = 56 << 20


def call(body, outs, scratch=(), flops=0, moved=0, name=None):
    return pl.pallas_call(
        body,
        out_shape=tuple(jax.ShapeDtypeStruct(shape, kind) for shape, kind in outs),
        scratch_shapes=list(scratch),
        compiler_params=pltpu.CompilerParams(vmem_limit_bytes=VMEM_LIMIT),
        cost_estimate=pl.CostEstimate(flops=flops, bytes_accessed=moved, transcendentals=0),
        name=name,
    )


def lane_of(shape):
    return lax.broadcasted_iota(jnp.int32, shape, 1)


def turn(values, amount):
    return pltpu.roll(values, amount % LANES, 1)


def weights_body(expand_one, reduce_one, pool, expand_two, reduce_two, first, second):
    hid_one, wide_one = (expand_one.shape[1], expand_one.shape[0])
    first[0:hid_one, 0:wide_one] = expand_one[...].T
    first[hid_one : hid_one + wide_one, :] = reduce_one[...].T
    base = hid_one + wide_one
    for quad in range(4):
        first[base + wide_one * quad : base + wide_one * (quad + 1), 0:wide_one] = pool[quad].T
    hid_two, wide_two = (expand_two.shape[1], expand_two.shape[0])
    second[0:hid_two, :] = expand_two[...].T
    for part in range(2):
        second[hid_two + wide_two * part : hid_two + wide_two * (part + 1), :] = reduce_two[
            wide_two * part : wide_two * (part + 1), :
        ].T


def pack_rows(read, places, group, left_out, right_out, channels):
    width = LANES // group
    for start in range(0, channels, 32):
        part = pl.ds(start, 32)
        lane = lane_of((32, LANES))
        left = jnp.zeros((32, LANES), F32)
        right = jnp.zeros((32, LANES), F32)
        for row, first, packed in places:
            values = read(row, part)
            inside = (lane >= SIDE * packed) & (lane < SIDE * packed + SIDE)
            left = jnp.where(inside, turn(values, SIDE * packed - first), left)
            last = first + width - SIDE
            right = jnp.where(inside, turn(values, SIDE * packed - last), right)
        left_out[part, :] = left.astype(BF16)
        right_out[part, :] = right.astype(BF16)


def assemble_one_body(own, sib, outer, whole, left_out, right_out):
    half = lax.axis_index("chan")
    count, group = (own.shape[0], own.shape[1])
    mine = pl.ds(pl.multiple_of(half * group, 16), group)
    other = pl.ds(pl.multiple_of((1 - half) * group, 16), group)
    rows = pl.ds(SIDE * (1 - half), count)
    edge = pl.ds(count * half, SIDE)
    whole[rows, mine, :] = own[...]
    whole[rows, other, :] = sib[...]
    whole[edge, other, :] = outer[:, 0:group, :]
    whole[edge, mine, :] = outer[:, group:, :]
    places = [(row, 0, row) for row in range(whole.shape[0])]
    pack_rows(lambda r, c: whole[r, c, :].astype(F32), places, 1, left_out, right_out, 2 * group)


def assemble_two_body(pooled, from_sib, from_outer, whole, left_out, right_out):
    top_is_outer = lax.axis_index("chan") == 0
    count, channels = (pooled.shape[0], pooled.shape[1])
    for row in range(count):
        whole[SIDE + row] = pooled[row]
    for start in range(0, channels, 64):
        part = pl.ds(start, 64)
        low = lane_of((64, LANES)) < LANES // 2

        def get(ref, row):
            return ref[row, part, :].astype(F32)

        sib0, sib1 = (get(from_sib, 0), get(from_sib, 1))
        out0, out1 = (get(from_outer, 0), get(from_outer, 1))
        top0, top1 = (jnp.where(top_is_outer, out0, sib0), jnp.where(top_is_outer, out1, sib1))
        low0, low1 = (jnp.where(top_is_outer, sib0, out0), jnp.where(top_is_outer, sib1, out1))
        above = (top0, turn(top0, 64), top1)
        below = (turn(low0, 64), low0, turn(low1, 64))
        for k in range(SIDE):
            mid = turn(get(pooled, count - SIDE + k), 64)
            whole[k, part, :] = jnp.where(low, above[k], mid).astype(BF16)
            mid = turn(get(pooled, k), 64)
            whole[SIDE + count + k, part, :] = jnp.where(low, mid, below[k]).astype(BF16)
    rows = count + 2 * SIDE
    places = [(k, 0, k) for k in range(rows)]
    places += [(k, 64, k + count) for k in range(rows - count, rows)]
    pack_rows(lambda r, c: whole[r, c, :].astype(F32), places, 2, left_out, right_out, channels)


def conv_body(whole, small_own, small_sib, out, taps, kbias):
    half = lax.axis_index("chan")
    rows, channels = (out.shape[0], out.shape[1])
    group = channels // 2
    for place, ref in ((half, small_own), (1 - half, small_sib)):
        part = pl.ds(pl.multiple_of(place * group, 16), group)
        columns = ref[...]
        for tap in range(TAPS * TAPS):
            taps[tap, part, :] = jnp.broadcast_to(
                columns[:, tap : tap + 1], (group, LANES)
            ).astype(BF16)
        kbias[part, :] = jnp.broadcast_to(
            columns[:, TAPS * TAPS : TAPS * TAPS + 1], (group, LANES)
        )
    blocks = channels // 16
    high = 8

    def step(index, carry):
        part = pl.ds(pl.multiple_of(lax.rem(index, blocks) * 16, 16), 16)
        start = lax.div(index, blocks) * high
        read = [whole[start + k, part, :] for k in range(high + TAPS - 1)]
        totals = [kbias[part, :] for _ in range(high)]
        for second in range(TAPS):
            column = [taps[TAPS * first + second, part, :] for first in range(TAPS)]
            for k in range(high):
                terms = [read[k + first] * column[first] for first in range(TAPS)]
                total = terms[0]
                for term in terms[1:]:
                    total = total + term
                total = total.astype(F32)
                if second != SIDE:
                    total = turn(total, SIDE - second)
                totals[k] = totals[k] + total
        for k in range(high):
            out[start + k, part, :] = totals[k].astype(BF16)
        return carry

    lax.fori_loop(0, blocks * (rows // high), step, 0)


def side_sums(left_in, right_in, left_own, right_own, small_own, small_sib, group, sums):
    half = lax.axis_index("chan")
    channels = left_in.shape[0]
    count = channels // 2
    for place, ref in ((half, small_own), (1 - half, small_sib)):
        part = pl.ds(pl.multiple_of(place * count, 16), count)
        lane = lane_of((count, LANES))
        column = lax.rem(lane, SIDE) if group == 1 else lax.rem(lax.rem(lane, 64), SIDE)
        pairs = ((left_in, right_own), (right_in, left_own))
        for side, (came, wrapped) in enumerate(pairs):
            fresh, stale = (came[part, :].astype(F32), wrapped[part, :].astype(F32))
            if group == 1:
                outside = fresh - stale
            else:
                upper = fresh - turn(stale, -24)
                lower = turn(turn(fresh, -24) - stale, 64)
                outside = jnp.where(lane < 64, upper, lower)
            total = jnp.zeros((count, LANES), F32)
            for near in range(SIDE):
                second = near if side == 0 else near + 4
                source = near if side == 0 else second - 6
                keep = (column + source >= 0) & (column + source < SIDE)
                partial = jnp.zeros((count, LANES), F32)
                for first in range(TAPS):
                    tap = TAPS * first + second
                    weight = ref[:, tap : tap + 1]
                    partial = partial + weight * turn(outside, -(SIDE * first + source))
                total = total + jnp.where(keep, partial, 0.0)
            sums[side, part, :] = total


def with_sides(mixed, sums, row, group):
    width = LANES // group
    lane = lane_of(mixed.shape)
    column = lane if group == 1 else lax.rem(lane, width)
    first = pltpu.roll(sums[0], LANES - SIDE * row, 1)
    last = pltpu.roll(sums[1], width - SIDE + (0 if group == 1 else LANES) - SIDE * row, 1)
    mixed = mixed + jnp.where(column < SIDE, first, 0.0)
    return mixed + jnp.where(column >= width - SIDE, last, 0.0)


def channel_norm(values, gain, shift):
    center = values - jnp.mean(values, axis=0, keepdims=True)
    spread = jnp.mean(center * center, axis=0, keepdims=True)
    return center * (lax.rsqrt(spread + 1e-06)) * gain + shift


def gelu(values):
    return 0.5 * values * (1.0 + lax.erf(values * 0.7071067811865476))


def dot(a, b):
    return jnp.dot(a, b, preferred_element_type=F32)


def bias_columns(ref, at, out, base):
    count = ref.shape[0]
    for k in range(4):
        out[base + count * k : base + count * (k + 1), :] = ref[:, at + k : at + k + 1]


def section_one_body(
    conv, whole, left_in, right_in, left_own, right_own, small_own, small_sib, vectors,
    weights_own, weights_sib, pbias_own, pbias_sib,
    out_own, out_sib, pooled, to_sib, to_outer,
    sums, quads, ebias,
):
    half = lax.axis_index("chan")
    rows, channels = (conv.shape[0], conv.shape[1])
    group = channels // 2
    hidden = weights_own.shape[1]
    side_sums(left_in, right_in, left_own, right_own, small_own, small_sib, 1, sums)
    bias_columns(small_own, TAPS * TAPS + 1, ebias, 0)
    bias_columns(small_sib, TAPS * TAPS + 1, ebias, hidden)
    even = lax.broadcasted_iota(jnp.int32, (2 * LANES, 2 * LANES), 0)
    to = lax.broadcasted_iota(jnp.int32, (2 * LANES, 2 * LANES), 1)
    source = 2 * lax.rem(to, LANES) + lax.div(to, LANES)
    pick = jnp.where(even == source, 1.0, 0.0).astype(BF16)
    lane = lane_of((channels, LANES))
    first_rows = rows // 2

    def step(index, carry):
        order = [2 * index, 2 * index + first_rows, 2 * index + 1, 2 * index + 1 + first_rows]
        gain, shift, rbias, scale = (vectors[:, k : k + 1] for k in range(4))
        pgain, pshift = (vectors[:, 4:5], vectors[:, 5:6])
        mixed = jnp.concatenate(
            [with_sides(conv[row].astype(F32), sums, row, 1) for row in order], axis=1
        )
        normed = channel_norm(mixed, gain, shift).astype(BF16)
        summed = None
        for place, ref in enumerate((weights_own, weights_sib)):
            inner = dot(ref[0:hidden, 0:channels], normed)
            inner = gelu(inner + ebias[hidden * place : hidden * (place + 1), :]).astype(BF16)
            term = dot(ref[hidden : hidden + channels, :], inner)
            summed = term if summed is None else summed + term
        base = jnp.concatenate([whole[row + SIDE].astype(F32) for row in order], axis=1)
        block = (base + scale * (summed + rbias)).astype(BF16)
        for k, row in enumerate(order):
            low = block[0:group, LANES * k : LANES * (k + 1)]
            top = block[group:, LANES * k : LANES * (k + 1)]
            out_own[row] = jnp.where(half == 0, low, top)
            out_sib[row] = jnp.where(half == 0, top, low)
        pnorm = channel_norm(block.astype(F32), pgain, pshift).astype(BF16)
        for down in range(2):
            parted = dot(pnorm[:, 2 * LANES * down : 2 * LANES * (down + 1)], pick).astype(BF16)
            at = pl.ds(pl.multiple_of(index * LANES, LANES), LANES)
            quads[2 * down, :, at] = parted[:, 0:LANES]
            quads[2 * down + 1, :, at] = parted[:, LANES:]
        return carry

    lax.fori_loop(0, rows // 4, step, 0)
    base = hidden + channels
    for place, ref, bias in ((half, weights_own, pbias_own), (1 - half, weights_sib, pbias_sib)):
        total = None
        for quad in range(4):
            term = dot(
                ref[base + channels * quad : base + channels * (quad + 1), 0:channels], quads[quad]
            )
            total = term if total is None else total + term
        total = (total + bias[...]).astype(BF16)
        part = pl.ds(pl.multiple_of(place * channels, 16), channels)
        for row in range(pooled.shape[0]):
            pooled[row, part, :] = total[:, LANES * row : LANES * (row + 1)]
    count = pooled.shape[0]
    for start in range(0, pooled.shape[1], 64):
        part = pl.ds(start, 64)
        low = lane_of((64, LANES)) < 64
        read = {k: pooled[k, part, :].astype(F32) for k in (0, 1, 2, count - 3, count - 2, count - 1)}
        top = (jnp.where(low, read[0], turn(read[1], 64)), read[2])
        bottom = (
            jnp.where(low, turn(read[count - 3], 64), read[count - 2]),
            turn(read[count - 1], 64),
        )
        for k in range(2):
            to_sib[k, part, :] = jnp.where(half == 0, bottom[k], top[k]).astype(BF16)
            to_outer[k, part, :] = jnp.where(half == 0, top[k], bottom[k]).astype(BF16)


def section_two_body(
    conv, whole, left_in, right_in, left_own, right_own, small_own, small_sib, vectors,
    weights_own, weights_sib,
    out_own, out_sib,
    sums, ebias,
):
    half = lax.axis_index("chan")
    rows, channels = (conv.shape[0], conv.shape[1])
    group = channels // 2
    hidden = 2 * channels
    side_sums(left_in, right_in, left_own, right_own, small_own, small_sib, 2, sums)
    bias_columns(small_own, TAPS * TAPS + 1, ebias, 0)
    bias_columns(small_sib, TAPS * TAPS + 1, ebias, hidden)

    def step(index, carry):
        order = [4 * index + k for k in range(4)]
        gain, shift, rbias, scale = (vectors[:, k : k + 1] for k in range(4))
        mixed = jnp.concatenate(
            [with_sides(conv[row].astype(F32), sums, row, 2) for row in order], axis=1
        )
        normed = channel_norm(mixed, gain, shift).astype(BF16)
        summed = None
        for place, ref in enumerate((weights_own, weights_sib)):
            for part in range(2):
                rows_of = channels * part
                inner = dot(ref[rows_of : rows_of + channels, :], normed)
                at = hidden * place + rows_of
                inner = gelu(inner + ebias[at : at + channels, :]).astype(BF16)
                term = dot(ref[hidden + rows_of : hidden + rows_of + channels, :], inner)
                summed = term if summed is None else summed + term
        base = jnp.concatenate([whole[row + SIDE].astype(F32) for row in order], axis=1)
        block = (base + scale * (summed + rbias)).astype(BF16)
        for k, row in enumerate(order):
            low = block[0:group, LANES * k : LANES * (k + 1)]
            top = block[group:, LANES * k : LANES * (k + 1)]
            out_own[row] = jnp.where(half == 0, low, top)
            out_sib[row] = jnp.where(half == 0, top, low)
        return carry

    lax.fori_loop(0, rows // 4, step, 0)


def on_device(
    image, kernel_one, kbias_one, gain_one, shift_one, expand_one, ebias_one, reduce_one,
    rbias_one, scale_one, pool_gain, pool_shift, pool_weight, pool_bias, kernel_two, kbias_two,
    gain_two, shift_two, expand_two, ebias_two, reduce_two, rbias_two, scale_two,
):
    half = lax.axis_index("chan")
    group, rows, cols = image.shape
    channels = 2 * group
    coarse_group = pool_weight.shape[2]
    coarse = 2 * coarse_group
    half_rows = rows // 2
    packed_rows = half_rows // 4
    n_row, n_col = (lax.axis_size("row"), lax.axis_size("col"))
    swap = [(0, 1), (1, 0)]
    outward = [(2 * r + 1, 2 * r + 2) for r in range(n_row - 1)]
    outward += [(b, a) for a, b in outward]
    right = [(c, c + 1) for c in range(n_col - 1)]
    left = [(b, a) for a, b in right]

    def to_sibling(x):
        return lax.ppermute(x, "chan", swap)

    def to_outer(x):
        return lax.ppermute(x, ("row", "chan"), outward)

    def sides(left_own, right_own):
        return (lax.ppermute(right_own, "col", right), lax.ppermute(left_own, "col", left))

    turned = image.transpose(1, 0, 2)
    span = half_rows + SIDE
    own = lax.dynamic_slice_in_dim(turned, (half_rows - SIDE) * half, span, 0)
    sib = to_sibling(lax.dynamic_slice_in_dim(turned, (half_rows - SIDE) * (1 - half), span, 0))

    first_shape = (expand_one.shape[1] + 5 * channels, expand_one.shape[1])
    second_shape = (2 * expand_two.shape[1], coarse)
    first_own, second_own = call(
        weights_body, [(first_shape, BF16), (second_shape, BF16)], name="turn_weights"
    )(expand_one, reduce_one, pool_weight, expand_two, reduce_two)
    small_one = jnp.concatenate(
        [kernel_one.reshape(group, -1), kbias_one[:, None], ebias_one.reshape(4, group).T], axis=1
    )
    small_two = jnp.concatenate(
        [
            kernel_two.reshape(coarse_group, -1),
            kbias_two[:, None],
            ebias_two.reshape(4, coarse_group).T,
            pool_bias[:, None],
        ],
        axis=1,
    )
    small = jnp.concatenate([jnp.pad(small_one, ((0, 0), (0, 1))), small_two], axis=0)
    small = jnp.pad(small, ((0, 0), (0, LANES - small.shape[1])))
    small_sib = to_sibling(small)
    first_sib = to_sibling(first_own)
    vectors_one = jnp.stack(
        [gain_one, shift_one, rbias_one, scale_one, pool_gain, pool_shift], axis=1
    )
    vectors_two = jnp.stack([gain_two, shift_two, rbias_two, scale_two], axis=1)

    edge = [lax.dynamic_slice_in_dim(x, half_rows * half, SIDE, 0) for x in (own, sib)]
    outer = to_outer(jnp.concatenate(edge, axis=1))
    side_shape = ((channels, LANES), BF16)
    whole, left_own, right_own = call(
        assemble_one_body,
        [((half_rows + 2 * SIDE, channels, LANES), BF16), side_shape, side_shape],
        name="assemble_one",
    )(own, sib, outer)
    left_in, right_in = sides(left_own, right_own)
    one_own, one_sib = (small[:group], small_sib[:group])
    (conv,) = call(
        conv_body,
        [((half_rows, channels, LANES), BF16)],
        [pltpu.VMEM((TAPS * TAPS, channels, LANES), BF16), pltpu.VMEM((channels, LANES), F32)],
        flops=10**10,
        moved=10**7,
        name="conv_one",
    )(whole, one_own, one_sib)
    message = ((2, coarse, LANES), BF16)
    block_shape = ((half_rows, group, LANES), BF16)
    block_own, block_sib, pooled, for_sib, for_outer = call(
        section_one_body,
        [block_shape, block_shape, ((packed_rows, coarse, LANES), BF16), message, message],
        [
            pltpu.VMEM((2, channels, LANES), F32),
            pltpu.VMEM((4, channels, LANES * packed_rows), BF16),
            pltpu.VMEM((2 * expand_one.shape[1], 1), F32),
        ],
        flops=10**10,
        moved=10**7,
        name="section_one",
    )(
        conv, whole, left_in, right_in, left_own, right_own, one_own, one_sib, vectors_one,
        first_own, first_sib, small[group:, 54:55], small_sib[group:, 54:55],
    )
    from_sib = to_sibling(for_sib)
    from_outer = to_outer(for_outer)
    second_sib = to_sibling(second_own)
    side_shape = ((coarse, LANES), BF16)
    whole_two, left_own, right_own = call(
        assemble_two_body,
        [((packed_rows + 2 * SIDE, coarse, LANES), BF16), side_shape, side_shape],
        name="assemble_two",
    )(pooled, from_sib, from_outer)
    left_in, right_in = sides(left_own, right_own)
    block_came = to_sibling(block_sib)
    two_own, two_sib = (small[group:], small_sib[group:])
    (conv,) = call(
        conv_body,
        [((packed_rows, coarse, LANES), BF16)],
        [pltpu.VMEM((TAPS * TAPS, coarse, LANES), BF16), pltpu.VMEM((coarse, LANES), F32)],
        flops=5 * 10**9,
        moved=10**7,
        name="conv_two",
    )(whole_two, two_own, two_sib)
    block_shape = ((packed_rows, coarse_group, LANES), BF16)
    two_block_own, two_block_sib = call(
        section_two_body,
        [block_shape, block_shape],
        [pltpu.VMEM((2, coarse, LANES), F32), pltpu.VMEM((2 * expand_two.shape[1], 1), F32)],
        flops=10**10,
        moved=10**7,
        name="section_two",
    )(
        conv, whole_two, left_in, right_in, left_own, right_own, two_own, two_sib, vectors_two,
        second_own, second_sib,
    )
    two_came = to_sibling(two_block_sib)

    def in_order(mine, came):
        return jnp.where(half == 0, jnp.stack([mine, came]), jnp.stack([came, mine]))

    block_one = in_order(block_own, block_came).reshape(rows, group, cols).transpose(1, 0, 2)
    both = in_order(two_block_own, two_came)
    both = both.reshape(2, packed_rows, coarse_group, 2, cols // 2).transpose(2, 0, 3, 1, 4)
    block_two = both.reshape(coarse_group, half_rows, cols // 2)
    return (block_one, block_two)


def solution(mesh):
    tile = P("chan", "row", "col")
    return jax.shard_map(
        on_device,
        mesh=mesh,
        in_specs=(
            tile, P("chan", None, None), P("chan"), P(), P(), P(None, "chan"), P("chan"),
            P("chan", None), P(), P(), P(), P(), P(None, None, "chan"), P("chan"),
            P("chan", None, None), P("chan"), P(), P(), P(None, "chan"), P("chan"),
            P("chan", None), P(), P(),
        ),
        out_specs=(tile, tile),
        check_vma=False,
    )
```

time: 423 us -> 132 us (0.31)
  the two profiles are of different devices: /device:TPU:1 before, /device:TPU:39 now
where the time goes in v1:
time: 132 us; the launch traced here: 131 us
  Pallas kernels  72.2 us (55%)
  starting transfers between devices  28.9 us (22%)
  local copies, waits for them, and re-layouts  20.1 us (15%)
  waiting for transfers between devices  8.31 us (6%)
    pallas_call x1, Pallas kernels, on_device(): call(section_one_body, [block_shape, block_shape, ((packed_rows, coarse,...  19.4 us
    pallas_call x1, Pallas kernels, on_device(): call(conv_body, [((half_rows, channels, LANES), BF16)], [pltpu.VMEM((TAPS...  16.2 us
    pallas_call x1, Pallas kernels, on_device(): call(section_two_body, [block_shape, block_shape], [pltpu.VMEM((2, coarse...  15.8 us
    ppermute x2, starting transfers between devices, to_outer(): return lax.ppermute(x, ('row', 'chan'), outward)  13.5 us
    pallas_call x1, Pallas kernels, on_device(): call(conv_body, [((packed_rows, coarse, LANES), BF16)], [pltpu.VMEM((TAPS...  10.1 us
    ppermute x2, waiting for transfers between devices, to_outer(): return lax.ppermute(x, ('row', 'chan'), outward)  7.56 us
    ppermute x2, starting transfers between devices, sides(): lax.ppermute(right_own, 'col', right)  6.79 us
    unnamed x60, local copies, waits for them, and re-layouts  6.36 us
  transfers between devices with their start and end apart: 13, of which 2 were waited for; matrix products, arithmetic and copies ran while one was open for 9% of the time, Pallas kernels for 55%

profile of v1, /device:TPU:39, one launch (start us, length us, event | category | flops | bytes accessed | tf_op | source)
XLA Modules:
  0.0 131.5 jit_solution(13793845061786048998)
XLA Ops:
  0.6 2.7 %constant_dynamic-slice_fusion.2 = (bf16[96,35,128]{2,1,0:T(8,128)(2,1)S(1)}, bf16[96,35,128]{2,1,0:T(8,128)(2,1)S(1)}) fusion(bf16[96,64,128]{2,1,0:T(8,128)(2,1)} %param.23, s32[]{:T(128)S(6)} %select_n.37, s32[]{:T(128)S(6)} %select_n.36), kind=kLoop, calls=%fused_computation.23 | loop fusion | bytes 3440648 | tf_op jit(solution)/shard_map/dynamic-slice.1
  3.4 0.1 copy.111
  3.5 0.8 collective-permute-start
  4.3 0.1 copy.94.pbias_own
  5.1 0.1 copy.91
  5.2 0.1 copy.93
  5.4 0.1 select_maximum_fusion
  5.6 0.5 collective-permute-start.2
  6.0 1.0 constant_dynamic-slice_fusion.1
  7.1 7.9 %collective-permute-start.1 = (bf16[3,192,128]{2,1,0:T(8,128)(2,1)S(1)}, bf16[3,192,128]{2,1,0:T(8,128)(2,1)S(1)}, u32[]{:S(2)}, u32[]{:S(2)}) collective-permute-start(bf16[3,192,128]{2,1,0:T(8,128)(2,1)S(1)} %pad_maximum_fusion), channel_id=1, source_target_pairs={{1,32},{33,64},{65,96},{97,128},{129,160},{161,192},{193,224},{32,... | collective-permute-start | bytes 442376 | tf_op jit(solution)/shard_map/ppermute | solution.py:356
  15.1 0.8 copy.95.reduce_one
  15.9 3.2 %turn_weights.1 = (bf16[1344,384]{1,0:T(8,128)(2,1)}, bf16[1536,384]{1,0:T(8,128)(2,1)}) custom-call(bf16[192,384]{1,0:T(8,128)(2,1)} %expand_one.1, bf16[384,192]{1,0:T(8,128)(2,1)} %copy.95.reduce_one, bf16[4,192,192]{2,1,0:T(8,128)(2,1)} %pool.1, bf16[384,768]{1,0:T(8,128)(2,1)} %expand_two.1, bf16[768,384]{1,0:T(8,128)(2,1)} %reduce_two.1), custom_call_target="tpu_custom_call" | custom-call | tf_op jit(solution)/shard_map/turn_weights/pallas_call | solution.py:368
  19.1 0.5 collective-permute-start.11
  19.7 0.6 slice.23.small_own
  20.3 1.0 copy.112
  21.4 0.8 copy.96.vectors
  22.1 0.6 slice.24.small_sib
  22.8 0.7 slice.25.pbias_sib
  23.5 0.7 copy-done.5
  24.2 3.8 %assemble_one.1 = (bf16[38,192,128]{2,1,0:T(8,128)(2,1)}, bf16[192,128]{1,0:T(8,128)(2,1)}, bf16[192,128]{1,0:T(8,128)(2,1)}) custom-call(bf16[35,96,128]{2,1,0:T(8,128)(2,1)} %bitcast.36, bf16[35,96,128]{2,1,0:T(8,128)(2,1)} %copy-done, bf16[3,192,128]{2,1,0:T(8,128)(2,1)} %copy-done.5), custom_call_target="tpu_custom_call" | custom-call | tf_op jit(solution)/shard_map/assemble_one/pallas_call | solution.py:395
  28.0 3.2 %collective-permute-start.3 = (bf16[192,128]{1,0:T(8,128)(2,1)}, bf16[192,128]{1,0:T(8,128)(2,1)S(1)}, u32[]{:S(2)}, u32[]{:S(2)}) collective-permute-start(bf16[192,128]{1,0:T(8,128)(2,1)} %get-tuple-element.18.right_own), channel_id=1, source_target_pairs={{0,2},{2,4},{4,6},{6,8},{8,10},{10,12},{12,14},{14,16},{16,18},{18... | collective-permute-start | bytes 147464 | tf_op jit(solution)/shard_map/ppermute | solution.py:359
  31.2 4.4 %collective-permute-start.4 = (bf16[192,128]{1,0:T(8,128)(2,1)}, bf16[192,128]{1,0:T(8,128)(2,1)S(1)}, u32[]{:S(2)}, u32[]{:S(2)}) collective-permute-start(bf16[192,128]{1,0:T(8,128)(2,1)} %get-tuple-element.19.left_own), channel_id=1, source_target_pairs={{2,0},{4,2},{6,4},{8,6},{10,8},{12,10},{14,12},{16,14},{18,16},{20... | collective-permute-start | bytes 147464 | tf_op jit(solution)/shard_map/ppermute | solution.py:359
  35.6 16.2 %conv_one.1.conv = bf16[32,192,128]{2,1,0:T(8,128)(2,1)} custom-call(bf16[38,192,128]{2,1,0:T(8,128)(2,1)} %get-tuple-element.17.whole, f32[96,128]{1,0:T(8,128)} %slice.23.small_own, f32[96,128]{1,0:T(8,128)} %slice.24.small_sib), custom_call_target="tpu_custom_call" | custom-call | flops 10000000000 | bytes 10000000 | tf_op jit(solution)/shard_map/conv_one/pallas_call | solution.py:402
  51.8 0.6 copy-done.26
  52.4 0.6 copy-done.27
  53.0 19.4 %section_one.1 = (bf16[32,96,128]{2,1,0:T(8,128)(2,1)}, bf16[32,96,128]{2,1,0:T(8,128)(2,1)}, bf16[8,384,128]{2,1,0:T(8,128)(2,1)}, bf16[2,384,128]{2,1,0:T(8,128)(2,1)}, bf16[2,384,128]{2,1,0:T(8,128)(2,1)}) custom-call(bf16[32,192,128]{2,1,0:T(8,128)(2,1)} %conv_one.1.conv, bf16[38,192,128]{2,1,0:T(8,128)(2,1)} %get-tuple-element.17.whole, ...), custom_call_target="tpu_custom_call" | custom-call | flops 10000000000 | bytes 10000000 | tf_op jit(solution)/shard_map/section_one/pallas_call | solution.py:412
  72.4 0.6 collective-permute-start.7
  73.1 5.5 %collective-permute-start.8 = (bf16[2,384,128]{2,1,0:T(8,128)(2,1)}, bf16[2,384,128]{2,1,0:T(8,128)(2,1)S(1)}, u32[]{:S(2)}, u32[]{:S(2)}) collective-permute-start(bf16[2,384,128]{2,1,0:T(8,128)(2,1)} %get-tuple-element.25), channel_id=1, source_target_pairs={{1,32},{33,64},{65,96},{97,128},{129,160},{161,192},{193,224},{32,... | collective-permute-start | bytes 589832 | tf_op jit(solution)/shard_map/ppermute | solution.py:356
  78.6 0.6 slice.26.small_own
  79.3 0.8 copy.99.vectors
  80.2 0.6 slice.27.small_sib
  80.8 7.6 %collective-permute-done.8.from_outer = bf16[2,384,128]{2,1,0:T(8,128)(2,1)S(1)} collective-permute-done((bf16[2,384,128]{2,1,0:T(8,128)(2,1)}, bf16[2,384,128]{2,1,0:T(8,128)(2,1)S(1)}, u32[]{:S(2)}, u32[]{:S(2)}) %collective-permute-start.8) | collective-permute-done | bytes 196640 | tf_op jit(solution)/shard_map/ppermute | solution.py:356
  88.4 0.7 copy-done.4
  89.1 3.7 %assemble_two.1 = (bf16[14,384,128]{2,1,0:T(8,128)(2,1)}, bf16[384,128]{1,0:T(8,128)(2,1)}, bf16[384,128]{1,0:T(8,128)(2,1)}) custom-call(bf16[8,384,128]{2,1,0:T(8,128)(2,1)} %get-tuple-element.23.pooled, bf16[2,384,128]{2,1,0:T(8,128)(2,1)} %copy-done.3, bf16[2,384,128]{2,1,0:T(8,128)(2,1)} %copy-done.4), custom_call_target="tpu_custom_call" | custom-call | tf_op jit(solution)/shard_map/assemble_two/pallas_call | solution.py:431
  92.8 1.9 %collective-permute-start.10 = (bf16[384,128]{1,0:T(8,128)(2,1)}, bf16[384,128]{1,0:T(8,128)(2,1)S(1)}, u32[]{:S(2)}, u32[]{:S(2)}) collective-permute-start(bf16[384,128]{1,0:T(8,128)(2,1)} %get-tuple-element.28.left_own), channel_id=1, source_target_pairs={{2,0},{4,2},{6,4},{8,6},{10,8},{12,10},{14,12},{16,14},{18,16},{20... | collective-permute-start | bytes 294920 | tf_op jit(solution)/shard_map/ppermute | solution.py:359
  94.7 3.6 %collective-permute-start.9 = (bf16[384,128]{1,0:T(8,128)(2,1)}, bf16[384,128]{1,0:T(8,128)(2,1)S(1)}, u32[]{:S(2)}, u32[]{:S(2)}) collective-permute-start(bf16[384,128]{1,0:T(8,128)(2,1)} %get-tuple-element.27.right_own), channel_id=1, source_target_pairs={{0,2},{2,4},{4,6},{6,8},{8,10},{10,12},{12,14},{14,16},{16,18},{18... | collective-permute-start | bytes 294920 | tf_op jit(solution)/shard_map/ppermute | solution.py:359
  98.3 10.1 %conv_two.1.conv = bf16[8,384,128]{2,1,0:T(8,128)(2,1)} custom-call(bf16[14,384,128]{2,1,0:T(8,128)(2,1)} %get-tuple-element.26.whole, f32[192,128]{1,0:T(8,128)} %slice.26.small_own, f32[192,128]{1,0:T(8,128)} %slice.27.small_sib), custom_call_target="tpu_custom_call" | custom-call | flops 5000000000 | bytes 10000000 | tf_op jit(solution)/shard_map/conv_two/pallas_call | solution.py:439
  108.4 0.6 copy-done.24
  109.0 0.6 copy-done.25
  109.7 15.8 %section_two.1 = (bf16[8,192,128]{2,1,0:T(8,128)(2,1)}, bf16[8,192,128]{2,1,0:T(8,128)(2,1)}) custom-call(bf16[8,384,128]{2,1,0:T(8,128)(2,1)} %conv_two.1.conv, bf16[14,384,128]{2,1,0:T(8,128)(2,1)} %get-tuple-element.26.whole, bf16[384,128]{1,0:T(8,128)(2,1)} %copy-done.25, bf16[384,128]{1,0:T(8,128)(2,1)} %copy-done.24, ...), custom_call_target="tpu_custom_call" | custom-call | flops 10000000000 | bytes 10000000 | tf_op jit(solution)/shard_map/section_two/pallas_call | solution.py:448
  125.5 1.2 copy.100
  126.7 0.7 collective-permute-done.12
  127.4 0.2 copy.101
  127.6 0.3 fusion
  128.0 1.0 copy.102
  129.0 0.4 copy-done.1
  129.5 0.3 maximum_select_fusion
  129.7 1.8 %copy.110 = bf16[64,96,128]{2,0,1:T(8,128)(2,1)} copy(bf16[64,96,128]{2,1,0:T(8,128)(2,1)S(1)} %bitcast.35) | data formatting | bytes 3145728 | tf_op jit(solution)/shard_map/jit(_where)/select_n | solution.py:462
  (81 shorter events, 0.9 us)
Async XLA Ops:
  3.3 1.0 copy-start.15
  3.3 1.1 copy-start.8
  3.3 1.2 copy-start.14
  3.3 1.4 %copy-start.23 = (f32[96]{0:T(128)S(1)}, f32[96]{0:T(128)}, u32[]{:S(2)}) copy-start(f32[96]{0:T(128)} %param.25) | copy-start | bytes 1156
  3.4 1.5 %copy-start.7 = (f32[192,7,7]{0,2,1:T(8,128)S(1)}, f32[192,7,7]{0,2,1:T(8,128)}, u32[]{:S(2)}) copy-start(f32[192,7,7]{0,2,1:T(8,128)} %param.37) | copy-start | bytes 112900
  3.4 1.6 %copy-start.9 = (f32[768]{0:T(1024)S(1)}, f32[768]{0:T(1024)}, u32[]{:S(2)}) copy-start(f32[768]{0:T(1024)} %param.42) | copy-start | bytes 9220
  3.4 1.8 %copy-start.16 = (f32[192]{0:T(256)S(1)}, f32[192]{0:T(256)}, u32[]{:S(2)}) copy-start(f32[192]{0:T(256)} %param.38) | copy-start | bytes 2308
  3.5 11.6 %copy-start.6 = (bf16[384,192]{0,1:T(8,128)(2,1)S(1)}, bf16[384,192]{0,1:T(8,128)(2,1)}, u32[]{:S(2)}) copy-start(bf16[384,192]{0,1:T(8,128)(2,1)} %param.30) | copy-start | bytes 442372
  3.5 3.5 %collective-permute-start = (bf16[35,96,128]{2,1,0:T(8,128)(2,1)S(1)}, bf16[35,96,128]{2,1,0:T(8,128)(2,1)S(1)}, u32[]{:S(2)}, u32[]{:S(2)}) collective-permute-start(bf16[35,96,128]{2,1,0:T(8,128)(2,1)S(1)} %bitcast.41), channel_id=1, source_target_pairs={{0,1},{1,0},{2,3},{3,2},{4,5},{5,4},{6,7},{7,6},{8,9},{9,8},{10,11... | collective-permute-start | bytes 2580488 | tf_op jit(solution)/shard_map/ppermute | solution.py:353
  4.4 14.7 %copy-start.2 = (f32[192,1]{1,0:T(8,128)}, f32[192,1]{1,0:T(8,128)S(1)}, u32[]{:S(2)}) copy-start(f32[192,1]{1,0:T(8,128)S(1)} %copy.94.pbias_own) | copy-start | bytes 2308
  5.6 16.6 %collective-permute-start.2 = (f32[288,128]{1,0:T(8,128)S(1)}, f32[288,128]{1,0:T(8,128)S(1)}, u32[]{:S(2)}, u32[]{:S(2)}) collective-permute-start(f32[288,128]{1,0:T(8,128)S(1)} %select_maximum_fusion), channel_id=1, source_target_pairs={{0,1},{1,0},{2,3},{3,2},{4,5},{5,4},{6,7},{7,6},{8,9},{9,8},{10,11... | collective-permute-start | bytes 442376 | tf_op jit(solution)/shard_map/ppermute | solution.py:353
  7.1 14.2 %copy-start = (bf16[35,96,128]{2,1,0:T(8,128)(2,1)}, bf16[35,96,128]{2,1,0:T(8,128)(2,1)S(1)}, u32[]{:S(2)}) copy-start(bf16[35,96,128]{2,1,0:T(8,128)(2,1)S(1)} %collective-permute-done.sib) | copy-start | bytes 2580484
  7.1 16.4 %collective-permute-start.1 = (bf16[3,192,128]{2,1,0:T(8,128)(2,1)S(1)}, bf16[3,192,128]{2,1,0:T(8,128)(2,1)S(1)}, u32[]{:S(2)}, u32[]{:S(2)}) collective-permute-start(bf16[3,192,128]{2,1,0:T(8,128)(2,1)S(1)} %pad_maximum_fusion), channel_id=1, source_target_pairs={{1,32},{33,64},{65,96},{97,128},{129,160},{161,192},{193,224},{32,... | collective-permute-start | bytes 442376 | tf_op jit(solution)/shard_map/ppermute | solution.py:356
  15.9 5.4 %copy-start.17 = (f32[192]{0:T(256)S(1)}, f32[192]{0:T(256)}, u32[]{:S(2)}) copy-start(f32[192]{0:T(256)} %param.26) | copy-start | bytes 2308
  15.9 5.4 %copy-start.18 = (f32[192]{0:T(256)S(1)}, f32[192]{0:T(256)}, u32[]{:S(2)}) copy-start(f32[192]{0:T(256)} %param.27) | copy-start | bytes 2308
  15.9 5.4 %copy-start.19 = (f32[192]{0:T(256)S(1)}, f32[192]{0:T(256)}, u32[]{:S(2)}) copy-start(f32[192]{0:T(256)} %param.31) | copy-start | bytes 2308
  15.9 5.4 %copy-start.20 = (f32[192]{0:T(256)S(1)}, f32[192]{0:T(256)}, u32[]{:S(2)}) copy-start(f32[192]{0:T(256)} %param.32) | copy-start | bytes 2308
  15.9 5.4 %copy-start.21 = (f32[192]{0:T(256)S(1)}, f32[192]{0:T(256)}, u32[]{:S(2)}) copy-start(f32[192]{0:T(256)} %param.33) | copy-start | bytes 2308
  15.9 5.4 %copy-start.22 = (f32[192]{0:T(256)S(1)}, f32[192]{0:T(256)}, u32[]{:S(2)}) copy-start(f32[192]{0:T(256)} %param.34) | copy-start | bytes 2308
  19.1 32.6 %collective-permute-start.5 = (bf16[1344,384]{1,0:T(8,128)(2,1)}, bf16[1344,384]{1,0:T(8,128)(2,1)}, u32[]{:S(2)}, u32[]{:S(2)}) collective-permute-start(bf16[1344,384]{1,0:T(8,128)(2,1)} %get-tuple-element.20.weights_own), channel_id=1, source_target_pairs={{0,1},{1,0},{2,3},{3,2},{4,5},{5,4},{6,7},{7,6},{8,9},{9,8},{10,11... | collective-permute-start | bytes 3096584 | tf_op jit(solution)/shard_map/ppermute | solution.py:353
  19.1 89.2 %collective-permute-start.11 = (bf16[1536,384]{1,0:T(8,128)(2,1)}, bf16[1536,384]{1,0:T(8,128)(2,1)}, u32[]{:S(2)}, u32[]{:S(2)}) collective-permute-start(bf16[1536,384]{1,0:T(8,128)(2,1)} %get-tuple-element.29.weights_own), channel_id=1, source_target_pairs={{0,1},{1,0},{2,3},{3,2},{4,5},{5,4},{6,7},{7,6},{8,9},{9,8},{10,11... | collective-permute-start | bytes 3538952 | tf_op jit(solution)/shard_map/ppermute | solution.py:353
  23.5 0.7 copy-start.5
  28.0 23.8 %collective-permute-start.3 = (bf16[192,128]{1,0:T(8,128)(2,1)}, bf16[192,128]{1,0:T(8,128)(2,1)S(1)}, u32[]{:S(2)}, u32[]{:S(2)}) collective-permute-start(bf16[192,128]{1,0:T(8,128)(2,1)} %get-tuple-element.18.right_own), channel_id=1, source_target_pairs={{0,2},{2,4},{4,6},{6,8},{8,10},{10,12},{12,14},{14,16},{16,18},{18... | collective-permute-start | bytes 147464 | tf_op jit(solution)/shard_map/ppermute | solution.py:359
  31.2 20.6 %collective-permute-start.4 = (bf16[192,128]{1,0:T(8,128)(2,1)}, bf16[192,128]{1,0:T(8,128)(2,1)S(1)}, u32[]{:S(2)}, u32[]{:S(2)}) collective-permute-start(bf16[192,128]{1,0:T(8,128)(2,1)} %get-tuple-element.19.left_own), channel_id=1, source_target_pairs={{2,0},{4,2},{6,4},{8,6},{10,8},{12,10},{14,12},{16,14},{18,16},{20... | collective-permute-start | bytes 147464 | tf_op jit(solution)/shard_map/ppermute | solution.py:359
  51.8 27.5 %copy-start.10 = (f32[384]{0:T(512)S(1)}, f32[384]{0:T(512)}, u32[]{:S(2)}) copy-start(f32[384]{0:T(512)} %param.39) | copy-start | bytes 4612
  51.8 27.5 %copy-start.11 = (f32[384]{0:T(512)S(1)}, f32[384]{0:T(512)}, u32[]{:S(2)}) copy-start(f32[384]{0:T(512)} %param.40) | copy-start | bytes 4612
  51.8 27.5 %copy-start.12 = (f32[384]{0:T(512)S(1)}, f32[384]{0:T(512)}, u32[]{:S(2)}) copy-start(f32[384]{0:T(512)} %param.44) | copy-start | bytes 4612
  51.8 27.5 %copy-start.13 = (f32[384]{0:T(512)S(1)}, f32[384]{0:T(512)}, u32[]{:S(2)}) copy-start(f32[384]{0:T(512)} %param.45) | copy-start | bytes 4612
  51.8 0.6 copy-start.26
  52.4 0.6 copy-start.27
  72.4 8.4 %collective-permute-start.7 = (bf16[2,384,128]{2,1,0:T(8,128)(2,1)}, bf16[2,384,128]{2,1,0:T(8,128)(2,1)S(1)}, u32[]{:S(2)}, u32[]{:S(2)}) collective-permute-start(bf16[2,384,128]{2,1,0:T(8,128)(2,1)} %get-tuple-element.24), channel_id=1, source_target_pairs={{0,1},{1,0},{2,3},{3,2},{4,5},{5,4},{6,7},{7,6},{8,9},{9,8},{10,11... | collective-permute-start | bytes 589832 | tf_op jit(solution)/shard_map/ppermute | solution.py:353
  73.1 15.3 %collective-permute-start.8 = (bf16[2,384,128]{2,1,0:T(8,128)(2,1)}, bf16[2,384,128]{2,1,0:T(8,128)(2,1)S(1)}, u32[]{:S(2)}, u32[]{:S(2)}) collective-permute-start(bf16[2,384,128]{2,1,0:T(8,128)(2,1)} %get-tuple-element.25), channel_id=1, source_target_pairs={{1,32},{33,64},{65,96},{97,128},{129,160},{161,192},{193,224},{32,... | collective-permute-start | bytes 589832 | tf_op jit(solution)/shard_map/ppermute | solution.py:356
  80.8 48.2 %collective-permute-start.6 = (bf16[32,96,128]{2,1,0:T(8,128)(2,1)}, bf16[32,96,128]{2,1,0:T(8,128)(2,1)S(1)}, u32[]{:S(2)}, u32[]{:S(2)}) collective-permute-start(bf16[32,96,128]{2,1,0:T(8,128)(2,1)} %get-tuple-element.22), channel_id=1, source_target_pairs={{0,1},{1,0},{2,3},{3,2},{4,5},{5,4},{6,7},{7,6},{8,9},{9,8},{10,11... | collective-permute-start | bytes 2359304 | tf_op jit(solution)/shard_map/ppermute | solution.py:353
  80.8 7.6 %copy-start.3 = (bf16[2,384,128]{2,1,0:T(8,128)(2,1)}, bf16[2,384,128]{2,1,0:T(8,128)(2,1)S(1)}, u32[]{:S(2)}) copy-start(bf16[2,384,128]{2,1,0:T(8,128)(2,1)S(1)} %collective-permute-done.7.from_sib) | copy-start | bytes 589828
  88.4 0.7 copy-start.4
  92.8 15.6 %collective-permute-start.10 = (bf16[384,128]{1,0:T(8,128)(2,1)}, bf16[384,128]{1,0:T(8,128)(2,1)S(1)}, u32[]{:S(2)}, u32[]{:S(2)}) collective-permute-start(bf16[384,128]{1,0:T(8,128)(2,1)} %get-tuple-element.28.left_own), channel_id=1, source_target_pairs={{2,0},{4,2},{6,4},{8,6},{10,8},{12,10},{14,12},{16,14},{18,16},{20... | collective-permute-start | bytes 294920 | tf_op jit(solution)/shard_map/ppermute | solution.py:359
  94.7 13.7 %collective-permute-start.9 = (bf16[384,128]{1,0:T(8,128)(2,1)}, bf16[384,128]{1,0:T(8,128)(2,1)S(1)}, u32[]{:S(2)}, u32[]{:S(2)}) collective-permute-start(bf16[384,128]{1,0:T(8,128)(2,1)} %get-tuple-element.27.right_own), channel_id=1, source_target_pairs={{0,2},{2,4},{4,6},{6,8},{8,10},{10,12},{12,14},{14,16},{16,18},{18... | collective-permute-start | bytes 294920 | tf_op jit(solution)/shard_map/ppermute | solution.py:359
  108.4 0.6 copy-start.24
  109.0 0.6 copy-start.25
  125.5 1.9 %collective-permute-start.12 = (bf16[8,192,128]{2,1,0:T(8,128)(2,1)}, bf16[8,192,128]{2,1,0:T(8,128)(2,1)S(1)}, u32[]{:S(2)}, u32[]{:S(2)}) collective-permute-start(bf16[8,192,128]{2,1,0:T(8,128)(2,1)} %get-tuple-element.31), channel_id=1, source_target_pairs={{0,1},{1,0},{2,3},{3,2},{4,5},{5,4},{6,7},{7,6},{8,9},{9,8},{10,11... | collective-permute-start | bytes 1179656 | tf_op jit(solution)/shard_map/ppermute | solution.py:353
  128.0 1.5 %copy-start.1 = (bf16[32,96,128]{2,1,0:T(8,128)(2,1)S(1)}, bf16[32,96,128]{2,1,0:T(8,128)(2,1)}, u32[]{:S(2)}) copy-start(bf16[32,96,128]{2,1,0:T(8,128)(2,1)} %get-tuple-element.21) | copy-start | bytes 2359300

commit v2 on v1

v2 whole, which is shorter than its diff:
```python
import functools

import jax
import jax.numpy as jnp
from jax import lax
from jax.experimental import pallas as pl
from jax.experimental.pallas import tpu as pltpu
from jax.sharding import PartitionSpec as P

F32 = jnp.float32
BF16 = jnp.bfloat16
LANES = 128
SIDE = 3
TAPS = 7
VMEM_LIMIT = 56 << 20
LINES = 16


def call(body, outs, scratch=(), flops=0, moved=0, name=None, ins=None):
    return pl.pallas_call(
        body,
        **({} if ins is None else {"grid": (1,), "in_specs": ins}),
        out_shape=tuple(jax.ShapeDtypeStruct(shape, kind) for shape, kind in outs),
        scratch_shapes=list(scratch),
        compiler_params=pltpu.CompilerParams(vmem_limit_bytes=VMEM_LIMIT),
        cost_estimate=pl.CostEstimate(flops=flops, bytes_accessed=moved, transcendentals=0),
        name=name,
    )


def lane_of(shape):
    return lax.broadcasted_iota(jnp.int32, shape, 1)


def turn(values, amount):
    return pltpu.roll(values, amount % LANES, 1)


def tap_table(kernel, stack):
    count = kernel.shape[2]
    stack[...] = jnp.zeros_like(stack)
    for first in range(TAPS):
        stack[TAPS * first : TAPS * (first + 1), 0:count] = kernel[first]
    return stack[...].T[0:count].astype(BF16)


def weights_body(
    expand_one, reduce_one, pool, expand_two, reduce_two, kernel_one, kernel_two, *rest
):
    lines, (out, stack, turned_one, turned_two) = (rest[:-4], rest[-4:])
    hid_one, wide_one = (expand_one.shape[1], expand_one.shape[0])
    hid_two, wide_two = (expand_two.shape[1], expand_two.shape[0])
    out[0:hid_one, 0:wide_one] = expand_one[...].T
    out[hid_one : hid_one + wide_one, :] = reduce_one[...]
    base = hid_one + wide_one
    for quad in range(4):
        out[base : base + wide_one, 0:wide_one] = pool[quad].T
        base += wide_one
    out[base : base + kernel_two.shape[2], 0:LANES] = tap_table(kernel_two, turned_two)
    base += kernel_two.shape[2]
    out[base : base + hid_two, :] = expand_two[...].T
    base += hid_two
    for part in range(2):
        out[base : base + wide_two, :] = reduce_two[wide_two * part : wide_two * (part + 1), :].T
        base += wide_two
    stack[...] = jnp.zeros_like(stack)
    at = 0
    for line in lines:
        row = line[...].reshape(1, line.shape[0])
        for start in range(0, line.shape[0], wide_two):
            piece = row[:, start : start + wide_two]
            stack[at : at + 1, 0 : piece.shape[1]] = piece
            at += 1
    values = stack[...].T
    for part in range(3):
        rounded = values.astype(BF16)
        out[base : base + wide_two, LANES * part : LANES * part + LINES] = rounded
        values = values - rounded.astype(F32)
    base += wide_two
    out[base : base + kernel_one.shape[2], 0:LANES] = tap_table(kernel_one, turned_one)


def columns_of(ref):
    first, second, third = (
        ref[:, LANES * part : LANES * part + LINES].astype(F32) for part in range(3)
    )
    return first + (second + third)


def row_place(row, group):
    per = LANES // group // (2 * SIDE)
    return row // per, 2 * SIDE * (row % per)


def pack_rows(whole, sides, group):
    rows, channels = (whole.shape[0], whole.shape[1])
    width = LANES // group

    def step(index, carry):
        part = pl.ds(pl.multiple_of(index * 16, 16), 16)
        column = lane_of((16, LANES)) & (width - 1)
        inside = (column < SIDE) | (column >= width - SIDE)
        keep = jnp.where(inside, 1.0, 0.0).astype(BF16)
        sums = [None] * (2 * (sides.shape[1] // LANES))
        for row in range(rows):
            which, place = row_place(row, group)
            term = turn(whole[row, part, :] * keep, place + SIDE)
            at = 2 * which + row % 2
            sums[at] = term if sums[at] is None else sums[at] + term
        for which in range(sides.shape[1] // LANES):
            sides[part, LANES * which : LANES * (which + 1)] = sums[2 * which] + sums[2 * which + 1]
        return carry

    lax.fori_loop(0, channels // 16, step, 0)


def assemble_one_body(own, sib, outer, whole, sides):
    half = lax.axis_index("chan")
    count, group = (own.shape[0], own.shape[1])
    mine = pl.ds(pl.multiple_of(half * group, 16), group)
    other = pl.ds(pl.multiple_of((1 - half) * group, 16), group)
    rows = pl.ds(SIDE * (1 - half), count)
    edge = pl.ds(count * half, SIDE)
    whole[rows, mine, :] = own[...]
    whole[rows, other, :] = sib[...]
    whole[edge, other, :] = outer[:, 0:group, :]
    whole[edge, mine, :] = outer[:, group:, :]
    pack_rows(whole, sides, 1)


def assemble_two_body(pooled, from_sib, from_outer, whole, sides):
    top_is_outer = lax.axis_index("chan") == 0
    count, channels = (pooled.shape[0], pooled.shape[1])
    group = from_sib.shape[1]
    for row in range(count):
        whole[SIDE + row] = pooled[row]
    for start in range(0, channels, group):
        part = pl.ds(start, group)
        low = lane_of((group, LANES)) < LANES // 2
        sib = [from_sib[4 * k + start // group] for k in range(2)]
        out = [from_outer[4 * k + start // group] for k in range(2)]
        top0, top1 = (jnp.where(top_is_outer, out[k], sib[k]) for k in range(2))
        low0, low1 = (jnp.where(top_is_outer, sib[k], out[k]) for k in range(2))
        above = (top0, turn(top0, 64), top1)
        below = (turn(low0, 64), low0, turn(low1, 64))
        for k in range(SIDE):
            mid = turn(pooled[count - SIDE + k, part, :], 64)
            whole[k, part, :] = jnp.where(low, above[k], mid)
            mid = turn(pooled[k, part, :], 64)
            whole[SIDE + count + k, part, :] = jnp.where(low, mid, below[k])
    pack_rows(whole, sides, 2)


def tap_columns(tables, columns, which, taps, kbias, channels):
    half = lax.axis_index("chan")
    group = channels // 2
    for place, table, column in zip((half, 1 - half), tables, columns):
        part = pl.ds(pl.multiple_of(place * group, 16), group)
        values = table[:, 0:LANES].astype(F32)
        for tap in range(TAPS * TAPS):
            one = values[:, tap : tap + 1]
            taps[tap, part, :] = jnp.broadcast_to(one, (group, LANES)).astype(BF16)
        kbias[part, :] = jnp.broadcast_to(column[0:group, which : which + 1], (group, LANES))


def convolve(whole, left_in, right_in, taps, kbias, out, edges, group, high):
    rows, channels = (out.shape[0], out.shape[1])
    width = LANES // group

    def step(index, carry):
        part = pl.ds(pl.multiple_of(index * 16, 16), 16)
        lane = lane_of((16, LANES))
        column = (lane & (width - 1)).astype(jnp.int16)
        first = jnp.where(lax.rem(lane & (width - 1), 2 * SIDE) < SIDE, 1.0, 0.0).astype(BF16)
        merged = [
            left_in[part, LANES * k : LANES * (k + 1)] * first
            + right_in[part, LANES * k : LANES * (k + 1)] * (1 - first)
            for k in range(left_in.shape[1] // LANES)
        ]
        for k in range(rows + 2 * SIDE):
            which, at = row_place(k, group)
            edges[k] = turn(merged[which], width - SIDE - at)
        for start in range(0, rows, high):
            totals = [kbias[part, :] for _ in range(high)]
            for second in range(TAPS):
                shift = SIDE - second
                read = [whole[start + k, part, :] for k in range(high + TAPS - 1)]
                if shift != 0:
                    outside = (
                        column >= jnp.int16(width - shift)
                        if shift > 0
                        else column < jnp.int16(-shift)
                    )
                    read = [
                        turn(jnp.where(outside, edges[start + k], read[k]), shift)
                        for k in range(high + TAPS - 1)
                    ]
                weights = [taps[TAPS * first + second, part, :] for first in range(TAPS)]
                for k in range(high):
                    total = read[k] * weights[0]
                    for first in range(1, TAPS):
                        total = total + read[k + first] * weights[first]
                    totals[k] = totals[k] + total.astype(F32)
            for k in range(high):
                out[start + k, part, :] = totals[k].astype(BF16)
        return carry

    lax.fori_loop(0, channels // 16, step, 0, unroll=group)


def channel_norm(values, gain, shift):
    center = values - jnp.mean(values, axis=0, keepdims=True)
    spread = jnp.mean(center * center, axis=0, keepdims=True)
    return center * (lax.rsqrt(spread + 1e-06)) * gain + shift


def gelu(values):
    return 0.5 * values * (1.0 + lax.erf(values * 0.7071067811865476))


def dot(a, b):
    return jnp.dot(a, b, preferred_element_type=F32)


def fetch(packed, start, into, flags):
    rows = into.shape[1]
    return [
        pltpu.make_async_copy(ref.at[pl.ds(start, rows)], into.at[k], flags.at[k])
        for k, ref in enumerate(packed)
    ]


def section_one_body(
    whole, left_in, right_in, taps_own, taps_sib, columns_own, columns_sib, packed_own, packed_sib,
    out_own, to_sib, pooled, to_outer,
    taps, kbias, edges, conv, quads, ebias, reduce, weights, flags,
):
    half = lax.axis_index("chan")
    rows, channels = (conv.shape[0], conv.shape[1])
    group = channels // 2
    hidden = weights.shape[2]
    copies = fetch((packed_own, packed_sib), 0, weights, flags)
    for copy in copies:
        copy.start()
    columns = (columns_of(columns_own), columns_of(columns_sib))
    tap_columns((taps_own, taps_sib), columns, 0, taps, kbias, channels)
    for place in range(2):
        ebias[hidden * place : hidden * (place + 1), :] = columns[place][:, 1:2]
    convolve(whole, left_in, right_in, taps, kbias, conv, edges, 1, 16)
    for place, copy in enumerate(copies):
        copy.wait()
        at = hidden * place
        reduce[:, at : at + hidden] = weights[place, hidden : hidden + channels, :]
    named = columns[0][0:channels]
    taken = lax.broadcasted_iota(jnp.int32, (2 * LANES, 2 * LANES), 0)
    to = lax.broadcasted_iota(jnp.int32, (2 * LANES, 2 * LANES), 1)
    source = 2 * lax.rem(to, LANES) + lax.div(to, LANES)
    pick = jnp.where(taken == source, 1.0, 0.0).astype(BF16)
    first_rows = rows // 2

    def step(index, carry):
        order = [2 * index, 2 * index + first_rows, 2 * index + 1, 2 * index + 1 + first_rows]
        gain, shift, rbias, scale = (named[:, k : k + 1] for k in range(6, 10))
        pgain, pshift = (named[:, 10:11], named[:, 11:12])
        mixed = jnp.concatenate([conv[row].astype(F32) for row in order], axis=1)
        normed = channel_norm(mixed, gain, shift).astype(BF16)
        inner = [
            gelu(
                dot(weights[place, 0:hidden, 0:channels], normed)
                + ebias[hidden * place : hidden * (place + 1), :]
            ).astype(BF16)
            for place in range(2)
        ]
        summed = dot(reduce[...], jnp.concatenate(inner, axis=0))
        base = jnp.concatenate([whole[row + SIDE].astype(F32) for row in order], axis=1)
        block = (base + scale * (summed + rbias)).astype(BF16)
        for k, row in enumerate(order):
            low = block[0:group, LANES * k : LANES * (k + 1)]
            top = block[group:, LANES * k : LANES * (k + 1)]
            out_own[row] = jnp.where(half == 0, low, top)
            to_sib[row] = jnp.where(half == 0, top, low)
        pnorm = channel_norm(block.astype(F32), pgain, pshift).astype(BF16)
        for down in range(2):
            parted = dot(pnorm[:, 2 * LANES * down : 2 * LANES * (down + 1)], pick).astype(BF16)
            at = pl.ds(pl.multiple_of(index * LANES, LANES), LANES)
            quads[2 * down, :, at] = parted[:, 0:LANES]
            quads[2 * down + 1, :, at] = parted[:, LANES:]
        return carry

    lax.fori_loop(0, rows // 4, step, 0)
    base = hidden + channels
    for slot, place in enumerate((half, 1 - half)):
        total = None
        for quad in range(4):
            at = base + channels * quad
            term = dot(weights[slot, at : at + channels, 0:channels], quads[quad])
            total = term if total is None else total + term
        total = (total + columns[slot][0:channels, 2:3]).astype(BF16)
        part = pl.ds(pl.multiple_of(place * channels, 16), channels)
        for row in range(pooled.shape[0]):
            pooled[row, part, :] = total[:, LANES * row : LANES * (row + 1)]
    count = pooled.shape[0]
    for start in range(0, pooled.shape[1], group):
        part = pl.ds(start, group)
        low = lane_of((group, LANES)) < 64
        read = {k: pooled[k, part, :] for k in (0, 1, 2, count - 3, count - 2, count - 1)}
        top = (jnp.where(low, read[0], turn(read[1], 64)), read[2])
        bottom = (
            jnp.where(low, turn(read[count - 3], 64), read[count - 2]),
            turn(read[count - 1], 64),
        )
        for k in range(2):
            to_sib[rows + 4 * k + start // group] = jnp.where(half == 0, bottom[k], top[k])
            to_outer[4 * k + start // group] = jnp.where(half == 0, top[k], bottom[k])


def section_two_body(
    whole, left_in, right_in, taps_own, taps_sib, columns_own, columns_sib, packed_own, packed_sib,
    out_own, out_sib,
    taps, kbias, edges, conv, ebias, reduce, weights, flags,
):
    half = lax.axis_index("chan")
    rows, channels = (conv.shape[0], conv.shape[1])
    group = channels // 2
    hidden = 2 * channels
    copies = fetch((packed_own, packed_sib), weights.shape[1], weights, flags)
    for copy in copies:
        copy.start()
    columns = (columns_of(columns_own), columns_of(columns_sib))
    tap_columns((taps_own, taps_sib), columns, 3, taps, kbias, channels)
    for place in range(2):
        for part in range(2):
            at = hidden * place + channels * part
            ebias[at : at + channels, :] = columns[place][:, 4 + part : 5 + part]
    convolve(whole, left_in, right_in, taps, kbias, conv, edges, 2, rows)
    for place, copy in enumerate(copies):
        copy.wait()
        for part in range(2):
            at = hidden * place + channels * part
            rows_of = hidden + channels * part
            reduce[:, at : at + channels] = weights[place, rows_of : rows_of + channels, :]
    named = columns[0]

    def step(index, carry):
        order = [4 * index + k for k in range(4)]
        gain, shift, rbias, scale = (named[:, k : k + 1] for k in range(12, 16))
        mixed = jnp.concatenate([conv[row].astype(F32) for row in order], axis=1)
        normed = channel_norm(mixed, gain, shift).astype(BF16)
        inner = [
            gelu(
                dot(weights[place, 0:hidden, :], normed) + ebias[hidden * place : hidden * (place + 1), :]
            ).astype(BF16)
            for place in range(2)
        ]
        summed = dot(reduce[...], jnp.concatenate(inner, axis=0))
        base = jnp.concatenate([whole[row + SIDE].astype(F32) for row in order], axis=1)
        block = (base + scale * (summed + rbias)).astype(BF16)
        for k, row in enumerate(order):
            low = block[0:group, LANES * k : LANES * (k + 1)]
            top = block[group:, LANES * k : LANES * (k + 1)]
            out_own[row] = jnp.where(half == 0, low, top)
            out_sib[row] = jnp.where(half == 0, top, low)
        return carry

    lax.fori_loop(0, rows // 4, step, 0)


def on_device(
    image, kernel_one, kbias_one, gain_one, shift_one, expand_one, ebias_one, reduce_one,
    rbias_one, scale_one, pool_gain, pool_shift, pool_weight, pool_bias, kernel_two, kbias_two,
    gain_two, shift_two, expand_two, ebias_two, reduce_two, rbias_two, scale_two,
):
    half = lax.axis_index("chan")
    group, rows, cols = image.shape
    channels = 2 * group
    coarse_group = pool_weight.shape[2]
    coarse = 2 * coarse_group
    half_rows = rows // 2
    packed_rows = half_rows // 4
    n_row, n_col = (lax.axis_size("row"), lax.axis_size("col"))
    swap = [(0, 1), (1, 0)]
    outward = [(2 * r + 1, 2 * r + 2) for r in range(n_row - 1)]
    outward += [(b, a) for a, b in outward]
    right = [(c, c + 1) for c in range(n_col - 1)]
    left = [(b, a) for a, b in right]

    def to_sibling(x):
        return lax.ppermute(x, "chan", swap)

    def to_outer(x):
        return lax.ppermute(x, ("row", "chan"), outward)

    def in_order(mine, came):
        return jnp.where(half == 0, jnp.stack([mine, came]), jnp.stack([came, mine]))

    def sides(own_sides):
        return (lax.ppermute(own_sides, "col", right), lax.ppermute(own_sides, "col", left))

    turned = image.transpose(1, 0, 2)
    span = half_rows + SIDE
    own = lax.dynamic_slice_in_dim(turned, (half_rows - SIDE) * half, span, 0)
    sib = to_sibling(lax.dynamic_slice_in_dim(turned, (half_rows - SIDE) * (1 - half), span, 0))

    hid_one, hid_two = (expand_one.shape[1], expand_two.shape[1])
    first_rows = hid_one + 5 * channels
    total_rows = first_rows + coarse_group + 2 * hid_two + coarse + group
    own, reduce_one = lax.optimization_barrier((own, reduce_one))
    (packed_own,) = call(
        weights_body,
        [((total_rows, coarse), BF16)],
        [
            pltpu.VMEM((LINES, coarse), F32),
            pltpu.VMEM((LANES, LANES), F32),
            pltpu.VMEM((LANES, 2 * LANES), F32),
        ],
        moved=10**7,
        name="turn_weights",
    )(
        expand_one, reduce_one.T, pool_weight, expand_two, reduce_two,
        kernel_one.transpose(1, 2, 0), kernel_two.transpose(1, 2, 0),
        kbias_one, ebias_one, pool_bias, kbias_two, ebias_two, gain_one, shift_one, rbias_one,
        scale_one, pool_gain, pool_shift, gain_two, shift_two, rbias_two, scale_two,
    )
    packed_sib = to_sibling(packed_own)

    def block(rows, start):
        return pl.BlockSpec((rows, coarse), lambda _: (start // rows, 0))

    taps_two_spec = block(coarse_group, first_rows)
    columns_spec = block(coarse, total_rows - group - coarse)
    taps_one_spec = block(group, total_rows - group)
    full = pl.BlockSpec(memory_space=pltpu.VMEM)
    there = pl.BlockSpec(memory_space=pl.ANY)

    edge = [lax.dynamic_slice_in_dim(x, half_rows * half, SIDE, 0) for x in (own, sib)]
    outer = to_outer(jnp.concatenate(edge, axis=1))
    side_shape = ((channels, 2 * LANES), BF16)
    whole, own_sides = call(
        assemble_one_body,
        [((half_rows + 2 * SIDE, channels, LANES), BF16), side_shape],
        name="assemble_one",
    )(own, sib, outer)
    left_in, right_in = sides(own_sides)
    message_rows = 2 * coarse // group

    def scratch_for(wide, high, hid, fetched):
        return [
            pltpu.VMEM((TAPS * TAPS, wide, LANES), BF16),
            pltpu.VMEM((wide, LANES), F32),
            pltpu.VMEM((high + 2 * SIDE, 16, LANES), BF16),
            pltpu.VMEM((high, wide, LANES), BF16),
        ], [
            pltpu.VMEM((2 * hid, 1), F32),
            pltpu.VMEM((wide, 2 * hid), BF16),
            pltpu.VMEM((2, fetched, coarse), BF16),
            pltpu.SemaphoreType.DMA((2,)),
        ]

    before, after = scratch_for(channels, half_rows, hid_one, first_rows)
    block_own, for_sib, pooled, for_outer = call(
        section_one_body,
        [
            ((half_rows, group, LANES), BF16),
            ((half_rows + message_rows, group, LANES), BF16),
            ((packed_rows, coarse, LANES), BF16),
            ((message_rows, group, LANES), BF16),
        ],
        before + [pltpu.VMEM((4, channels, LANES * packed_rows), BF16)] + after,
        flops=10**10,
        moved=10**7,
        name="section_one",
        ins=[full] * 3 + [taps_one_spec] * 2 + [columns_spec] * 2 + [there] * 2,
    )(whole, left_in, right_in, *[packed_own, packed_sib] * 3)
    from_sib = to_sibling(for_sib)
    from_outer = to_outer(for_outer)
    block_came = from_sib[:half_rows]
    side_shape = ((coarse, 2 * LANES), BF16)
    whole_two, own_sides = call(
        assemble_two_body,
        [((packed_rows + 2 * SIDE, coarse, LANES), BF16), side_shape],
        name="assemble_two",
        ins=[full, pl.BlockSpec((message_rows, group, LANES), lambda _: (half_rows // message_rows, 0, 0)), full],
    )(pooled, from_sib, from_outer)
    left_in, right_in = sides(own_sides)
    block_one = in_order(block_own, block_came).reshape(rows, group, cols).transpose(1, 0, 2)
    whole_two, block_one = lax.optimization_barrier((whole_two, block_one))
    before, after = scratch_for(coarse, packed_rows, hid_two, 2 * hid_two)
    block_shape = ((packed_rows, coarse_group, LANES), BF16)
    two_block_own, two_block_sib = call(
        section_two_body,
        [block_shape, block_shape],
        before + after,
        flops=10**10,
        moved=10**7,
        name="section_two",
        ins=[full] * 3 + [taps_two_spec] * 2 + [columns_spec] * 2 + [there] * 2,
    )(whole_two, left_in, right_in, *[packed_own, packed_sib] * 3)
    two_came = to_sibling(two_block_sib)

    both = in_order(two_block_own, two_came)
    both = both.reshape(2, packed_rows, coarse_group, 2, cols // 2).transpose(2, 0, 3, 1, 4)
    block_two = both.reshape(coarse_group, half_rows, cols // 2)
    return (block_one, block_two)


def solution(mesh):
    tile = P("chan", "row", "col")
    return jax.shard_map(
        on_device,
        mesh=mesh,
        in_specs=(
            tile, P("chan", None, None), P("chan"), P(), P(), P(None, "chan"), P("chan"),
            P("chan", None), P(), P(), P(), P(), P(None, None, "chan"), P("chan"),
            P("chan", None, None), P("chan"), P(), P(), P(None, "chan"), P("chan"),
            P("chan", None), P(), P(),
        ),
        out_specs=(tile, tile),
        check_vma=False,
    )
```

time: 132 us -> 123 us (0.932)
  the two profiles are of different devices: /device:TPU:39 before, /device:TPU:225 now
where the time goes in v2:
time: 123 us
  Pallas kernels  51.9 us (42%)
  starting transfers between devices  36.1 us (29%)
  waiting for transfers between devices  22.2 us (18%)
  local copies, waits for them, and re-layouts  11.3 us (9%)
    pallas_call x1, Pallas kernels, on_device(): call(section_one_body, [((half_rows, group, LANES), BF16), ((half_rows +...  23.9 us
    ppermute x4, starting transfers between devices, to_sibling(): return lax.ppermute(x, 'chan', swap)  18.6 us
    pallas_call x1, Pallas kernels, on_device(): call(section_two_body, [block_shape, block_shape], before + after, flops=...  14.7 us
    ppermute x2, waiting for transfers between devices, to_outer(): return lax.ppermute(x, ('row', 'chan'), outward)  8.59 us
    ppermute x2, waiting for transfers between devices, sides(): lax.ppermute(own_sides, 'col', right)  7.69 us
    ppermute x2, starting transfers between devices, sides(): lax.ppermute(own_sides, 'col', left)  6.98 us
    ppermute x4, waiting for transfers between devices, to_sibling(): return lax.ppermute(x, 'chan', swap)  5.89 us
    ppermute x2, starting transfers between devices, sides(): lax.ppermute(own_sides, 'col', right)  5.46 us
  transfers between devices with their start and end apart: 10, of which 6 were waited for; matrix products, arithmetic and copies ran while one was open for 4% of the time, Pallas kernels for 3%

profile of v2, /device:TPU:225, one launch (start us, length us, event | category | flops | bytes accessed | tf_op | source)
XLA Modules:
  0.0 123.0 jit_solution(13478150111319814688)
XLA Ops:
  0.6 2.7 %constant_dynamic-slice_fusion.2 = (bf16[96,35,128]{2,1,0:T(8,128)(2,1)S(1)}, bf16[96,35,128]{2,1,0:T(8,128)(2,1)S(1)}) fusion(bf16[96,64,128]{2,1,0:T(8,128)(2,1)} %param.23, s32[]{:T(128)S(6)} %select_n.32, s32[]{:T(128)S(6)} %select_n.31), kind=kLoop, calls=%fused_computation.10 | loop fusion | bytes 3440648 | tf_op jit(solution)/shard_map/dynamic-slice.1
  3.3 0.1 copy.47
  3.4 0.0 copy-start
  3.4 4.1 %turn_weights.1.taps_own.columns_own.packed_own = bf16[3552,384]{1,0:T(8,128)(2,1)} custom-call(bf16[192,384]{1,0:T(8,128)(2,1)} %expand_one.1, bf16[192,384]{1,0:T(8,128)(2,1)} %bitcast.30, bf16[4,192,192]{2,1,0:T(8,128)(2,1)} %pool.1, bf16[384,768]{1,0:T(8,128)(2,1)} %expand_two.1, bf16[768,384]{1,0:T(8,128)(2,1)} %reduce_two.1, f32[7,7,96]{2,1,0:T(8,128)} %bitcast.32, ...), custom_call_target="tpu_custom_call" | custom-call | bytes 10000000 | tf_op jit(solution)/shard_map/turn_weights/pallas_call | solution.py:408
  7.6 0.7 collective-permute-start.4
  8.3 0.1 copy.46
  8.4 0.1 collective-permute-start
  8.5 0.0 copy-done
  8.5 5.5 %collective-permute-done.sib = bf16[35,96,128]{2,1,0:T(8,128)(2,1)S(1)} collective-permute-done((bf16[35,96,128]{2,1,0:T(8,128)(2,1)S(1)}, bf16[35,96,128]{2,1,0:T(8,128)(2,1)S(1)}, u32[]{:S(2)}, u32[]{:S(2)}) %collective-permute-start) | collective-permute-done | bytes 860192 | tf_op jit(solution)/shard_map/ppermute | solution.py:388
  14.0 0.0 copy-start.2
  14.1 3.1 %collective-permute-start.1 = (bf16[3,192,128]{2,1,0:T(8,128)(2,1)S(1)}, bf16[3,192,128]{2,1,0:T(8,128)(2,1)S(1)}, u32[]{:S(2)}, u32[]{:S(2)}) collective-permute-start(bf16[3,192,128]{2,1,0:T(8,128)(2,1)S(1)} %pad_maximum_fusion), channel_id=1, source_target_pairs={{1,32},{33,64},{65,96},{97,128},{129,160},{161,192},{193,224},{32,... | collective-permute-start | bytes 442376 | tf_op jit(solution)/shard_map/ppermute | solution.py:391
  17.2 3.3 %collective-permute-done.1.outer = bf16[3,192,128]{2,1,0:T(8,128)(2,1)S(1)} collective-permute-done((bf16[3,192,128]{2,1,0:T(8,128)(2,1)S(1)}, bf16[3,192,128]{2,1,0:T(8,128)(2,1)S(1)}, u32[]{:S(2)}, u32[]{:S(2)}) %collective-permute-start.1) | collective-permute-done | bytes 147488 | tf_op jit(solution)/shard_map/ppermute | solution.py:391
  20.5 0.0 copy-done.2
  20.5 0.6 copy-done.5
  21.2 4.2 %assemble_one.1 = (bf16[38,192,128]{2,1,0:T(8,128)(2,1)}, bf16[192,256]{1,0:T(8,128)(2,1)}) custom-call(bf16[35,96,128]{2,1,0:T(8,128)(2,1)} %bitcast.23, bf16[35,96,128]{2,1,0:T(8,128)(2,1)} %copy-done.2, bf16[3,192,128]{2,1,0:T(8,128)(2,1)} %copy-done.5), custom_call_target="tpu_custom_call" | custom-call | tf_op jit(solution)/shard_map/assemble_one/pallas_call | solution.py:438
  25.3 5.1 %collective-permute-start.3 = (bf16[192,256]{1,0:T(8,128)(2,1)}, bf16[192,256]{1,0:T(8,128)(2,1)S(1)}, u32[]{:S(2)}, u32[]{:S(2)}) collective-permute-start(bf16[192,256]{1,0:T(8,128)(2,1)} %get-tuple-element.18), channel_id=1, source_target_pairs={{2,0},{4,2},{6,4},{8,6},{10,8},{12,10},{14,12},{16,14},{18,16},{20... | collective-permute-start | bytes 294920 | tf_op jit(solution)/shard_map/ppermute | solution.py:397
  30.4 1.9 %collective-permute-start.2 = (bf16[192,256]{1,0:T(8,128)(2,1)}, bf16[192,256]{1,0:T(8,128)(2,1)S(1)}, u32[]{:S(2)}, u32[]{:S(2)}) collective-permute-start(bf16[192,256]{1,0:T(8,128)(2,1)} %get-tuple-element.18), channel_id=1, source_target_pairs={{0,2},{2,4},{4,6},{6,8},{8,10},{10,12},{12,14},{14,16},{16,18},{18... | collective-permute-start | bytes 294920 | tf_op jit(solution)/shard_map/ppermute | solution.py:397
  32.3 0.0 collective-permute-done.3.right_in
  32.4 0.0 copy-start.8
  32.4 5.7 %collective-permute-done.2.left_in = bf16[192,256]{1,0:T(8,128)(2,1)S(1)} collective-permute-done((bf16[192,256]{1,0:T(8,128)(2,1)}, bf16[192,256]{1,0:T(8,128)(2,1)S(1)}, u32[]{:S(2)}, u32[]{:S(2)}) %collective-permute-start.2) | collective-permute-done | bytes 98336 | tf_op jit(solution)/shard_map/ppermute | solution.py:397
  38.1 0.0 collective-permute-done.4.taps_sib.columns_sib.packed_sib
  38.1 0.0 copy-done.8
  38.1 0.6 copy-done.9
  38.7 23.9 %section_one.1 = (bf16[32,96,128]{2,1,0:T(8,128)(2,1)}, bf16[40,96,128]{2,1,0:T(8,128)(2,1)}, bf16[8,384,128]{2,1,0:T(8,128)(2,1)}, bf16[8,96,128]{2,1,0:T(8,128)(2,1)}) custom-call(bf16[38,192,128]{2,1,0:T(8,128)(2,1)} %get-tuple-element.17.whole, bf16[192,256]{1,0:T(8,128)(2,1)} %copy-done.9, bf16[192,256]{1,0:T(8,128)(2,1)} %copy-done.8, ...), custom_call_target="tpu_custom_call" | custom-call | flops 10000000000 | bytes 10000000 | tf_op jit(solution)/shard_map/section_one/pallas_call | solution.py:460
  62.7 9.2 %collective-permute-start.5 = (bf16[40,96,128]{2,1,0:T(8,128)(2,1)}, bf16[40,96,128]{2,1,0:T(8,128)(2,1)S(1)}, u32[]{:S(2)}, u32[]{:S(2)}) collective-permute-start(bf16[40,96,128]{2,1,0:T(8,128)(2,1)} %get-tuple-element.21), channel_id=1, source_target_pairs={{0,1},{1,0},{2,3},{3,2},{4,5},{5,4},{6,7},{7,6},{8,9},{9,8},{10,11... | collective-permute-start | bytes 2949128 | tf_op jit(solution)/shard_map/ppermute | solution.py:388
  71.9 1.9 %collective-permute-start.6 = (bf16[8,96,128]{2,1,0:T(8,128)(2,1)}, bf16[8,96,128]{2,1,0:T(8,128)(2,1)S(1)}, u32[]{:S(2)}, u32[]{:S(2)}) collective-permute-start(bf16[8,96,128]{2,1,0:T(8,128)(2,1)} %get-tuple-element.22), channel_id=1, source_target_pairs={{1,32},{33,64},{65,96},{97,128},{129,160},{161,192},{193,224},{32,... | collective-permute-start | bytes 589832 | tf_op jit(solution)/shard_map/ppermute | solution.py:391
  73.9 5.3 %collective-permute-done.6.from_outer = bf16[8,96,128]{2,1,0:T(8,128)(2,1)S(1)} collective-permute-done((bf16[8,96,128]{2,1,0:T(8,128)(2,1)}, bf16[8,96,128]{2,1,0:T(8,128)(2,1)S(1)}, u32[]{:S(2)}, u32[]{:S(2)}) %collective-permute-start.6) | collective-permute-done | bytes 196640 | tf_op jit(solution)/shard_map/ppermute | solution.py:391
  79.1 0.0 collective-permute-done.5.from_sib
  79.1 0.7 copy-done.4
  79.8 0.3 copy-done.1
  80.1 4.9 %assemble_two.1 = (bf16[14,384,128]{2,1,0:T(8,128)(2,1)}, bf16[384,256]{1,0:T(8,128)(2,1)}) custom-call(bf16[8,384,128]{2,1,0:T(8,128)(2,1)} %get-tuple-element.20.pooled, bf16[40,96,128]{2,1,0:T(8,128)(2,1)} %copy-done.1, bf16[8,96,128]{2,1,0:T(8,128)(2,1)} %copy-done.4), custom_call_target="tpu_custom_call" | custom-call | tf_op jit(solution)/shard_map/assemble_two/pallas_call | solution.py:478
  85.1 1.9 %collective-permute-start.8 = (bf16[384,256]{1,0:T(8,128)(2,1)}, bf16[384,256]{1,0:T(8,128)(2,1)S(1)}, u32[]{:S(2)}, u32[]{:S(2)}) collective-permute-start(bf16[384,256]{1,0:T(8,128)(2,1)} %get-tuple-element.27), channel_id=1, source_target_pairs={{2,0},{4,2},{6,4},{8,6},{10,8},{12,10},{14,12},{16,14},{18,16},{20... | collective-permute-start | bytes 589832 | tf_op jit(solution)/shard_map/ppermute | solution.py:397
  87.0 3.5 %collective-permute-start.7 = (bf16[384,256]{1,0:T(8,128)(2,1)}, bf16[384,256]{1,0:T(8,128)(2,1)S(1)}, u32[]{:S(2)}, u32[]{:S(2)}) collective-permute-start(bf16[384,256]{1,0:T(8,128)(2,1)} %get-tuple-element.27), channel_id=1, source_target_pairs={{0,2},{2,4},{4,6},{6,8},{8,10},{10,12},{12,14},{14,16},{16,18},{18... | collective-permute-start | bytes 589832 | tf_op jit(solution)/shard_map/ppermute | solution.py:397
  90.6 1.2 slice_bitcast_fusion
  91.7 0.0 copy-done.3
  91.8 0.3 maximum_select_fusion
  92.0 1.8 %copy.45 = bf16[64,96,128]{2,0,1:T(8,128)(2,1)} copy(bf16[64,96,128]{2,1,0:T(8,128)(2,1)S(1)} %bitcast.21) | data formatting | bytes 3145728 | tf_op jit(solution)/shard_map/jit(_where)/select_n | solution.py:394
  93.8 0.0 collective-permute-done.8.right_in
  93.8 2.0 %collective-permute-done.7.left_in = bf16[384,256]{1,0:T(8,128)(2,1)S(1)} collective-permute-done((bf16[384,256]{1,0:T(8,128)(2,1)}, bf16[384,256]{1,0:T(8,128)(2,1)S(1)}, u32[]{:S(2)}, u32[]{:S(2)}) %collective-permute-start.7) | collective-permute-done | bytes 196640 | tf_op jit(solution)/shard_map/ppermute | solution.py:397
  95.7 0.0 copy-done.6
  95.7 0.7 copy-done.7
  96.4 14.7 %section_two.1 = (bf16[8,192,128]{2,1,0:T(8,128)(2,1)}, bf16[8,192,128]{2,1,0:T(8,128)(2,1)}) custom-call(bf16[14,384,128]{2,1,0:T(8,128)(2,1)} %get-tuple-element.26.whole, bf16[384,256]{1,0:T(8,128)(2,1)} %copy-done.7, bf16[384,256]{1,0:T(8,128)(2,1)} %copy-done.6, bf16[3552,384]{1,0:T(8,128)(2,1)} %turn_weights.1.taps_own.columns_own.packed_own, ...), custom_call_target="tpu_custom_call" | custom-call | flops 10000000000 | bytes 10000000 | tf_op jit(solution)/shard_map/section_two/pallas_call | solution.py:489
  111.2 8.6 %collective-permute-start.9 = (bf16[8,192,128]{2,1,0:T(8,128)(2,1)}, bf16[8,192,128]{2,1,0:T(8,128)(2,1)S(1)}, u32[]{:S(2)}, u32[]{:S(2)}) collective-permute-start(bf16[8,192,128]{2,1,0:T(8,128)(2,1)} %get-tuple-element.29), channel_id=1, source_target_pairs={{0,1},{1,0},{2,3},{3,2},{4,5},{5,4},{6,7},{7,6},{8,9},{9,8},{10,11... | collective-permute-start | bytes 1179656 | tf_op jit(solution)/shard_map/ppermute | solution.py:388
  119.8 1.2 copy.37
  121.0 0.4 collective-permute-done.9
  121.4 0.2 copy.38
  121.6 0.3 fusion
  121.9 1.0 copy.39
  (10 shorter events, 0.0 us)
Async XLA Ops:
  3.4 5.0 %copy-start = (bf16[96,35,128]{2,0,1:T(8,128)(2,1)}, bf16[96,35,128]{2,0,1:T(8,128)(2,1)S(1)}, u32[]{:S(2)}) copy-start(bf16[96,35,128]{2,0,1:T(8,128)(2,1)S(1)} %copy.47) | copy-start | bytes 2580484
  7.6 30.5 %collective-permute-start.4 = (bf16[3552,384]{1,0:T(8,128)(2,1)}, bf16[3552,384]{1,0:T(8,128)(2,1)}, u32[]{:S(2)}, u32[]{:S(2)}) collective-permute-start(bf16[3552,384]{1,0:T(8,128)(2,1)} %turn_weights.1.taps_own.columns_own.packed_own), channel_id=1, source_target_pairs={{0,1},{1,0},{2,3},{3,2},{4,5},{5,4},{6,7},{7,6},{8,9},{9,8},{10,11... | collective-permute-start | bytes 8183816 | tf_op jit(solution)/shard_map/ppermute | solution.py:388
  8.4 5.7 %collective-permute-start = (bf16[35,96,128]{2,1,0:T(8,128)(2,1)S(1)}, bf16[35,96,128]{2,1,0:T(8,128)(2,1)S(1)}, u32[]{:S(2)}, u32[]{:S(2)}) collective-permute-start(bf16[35,96,128]{2,1,0:T(8,128)(2,1)S(1)} %bitcast.28), channel_id=1, source_target_pairs={{0,1},{1,0},{2,3},{3,2},{4,5},{5,4},{6,7},{7,6},{8,9},{9,8},{10,11... | collective-permute-start | bytes 2580488 | tf_op jit(solution)/shard_map/ppermute | solution.py:388
  14.0 6.5 %copy-start.2 = (bf16[35,96,128]{2,1,0:T(8,128)(2,1)}, bf16[35,96,128]{2,1,0:T(8,128)(2,1)S(1)}, u32[]{:S(2)}) copy-start(bf16[35,96,128]{2,1,0:T(8,128)(2,1)S(1)} %collective-permute-done.sib) | copy-start | bytes 2580484
  14.1 6.5 %collective-permute-start.1 = (bf16[3,192,128]{2,1,0:T(8,128)(2,1)S(1)}, bf16[3,192,128]{2,1,0:T(8,128)(2,1)S(1)}, u32[]{:S(2)}, u32[]{:S(2)}) collective-permute-start(bf16[3,192,128]{2,1,0:T(8,128)(2,1)S(1)} %pad_maximum_fusion), channel_id=1, source_target_pairs={{1,32},{33,64},{65,96},{97,128},{129,160},{161,192},{193,224},{32,... | collective-permute-start | bytes 442376 | tf_op jit(solution)/shard_map/ppermute | solution.py:391
  20.5 0.6 copy-start.5
  25.3 7.0 %collective-permute-start.3 = (bf16[192,256]{1,0:T(8,128)(2,1)}, bf16[192,256]{1,0:T(8,128)(2,1)S(1)}, u32[]{:S(2)}, u32[]{:S(2)}) collective-permute-start(bf16[192,256]{1,0:T(8,128)(2,1)} %get-tuple-element.18), channel_id=1, source_target_pairs={{2,0},{4,2},{6,4},{8,6},{10,8},{12,10},{14,12},{16,14},{18,16},{20... | collective-permute-start | bytes 294920 | tf_op jit(solution)/shard_map/ppermute | solution.py:397
  30.4 7.7 %collective-permute-start.2 = (bf16[192,256]{1,0:T(8,128)(2,1)}, bf16[192,256]{1,0:T(8,128)(2,1)S(1)}, u32[]{:S(2)}, u32[]{:S(2)}) collective-permute-start(bf16[192,256]{1,0:T(8,128)(2,1)} %get-tuple-element.18), channel_id=1, source_target_pairs={{0,2},{2,4},{4,6},{6,8},{8,10},{10,12},{12,14},{14,16},{16,18},{18... | collective-permute-start | bytes 294920 | tf_op jit(solution)/shard_map/ppermute | solution.py:397
  32.4 5.8 %copy-start.8 = (bf16[192,256]{1,0:T(8,128)(2,1)}, bf16[192,256]{1,0:T(8,128)(2,1)S(1)}, u32[]{:S(2)}) copy-start(bf16[192,256]{1,0:T(8,128)(2,1)S(1)} %collective-permute-done.3.right_in) | copy-start | bytes 294916
  38.1 0.6 copy-start.9
  62.7 16.4 %collective-permute-start.5 = (bf16[40,96,128]{2,1,0:T(8,128)(2,1)}, bf16[40,96,128]{2,1,0:T(8,128)(2,1)S(1)}, u32[]{:S(2)}, u32[]{:S(2)}) collective-permute-start(bf16[40,96,128]{2,1,0:T(8,128)(2,1)} %get-tuple-element.21), channel_id=1, source_target_pairs={{0,1},{1,0},{2,3},{3,2},{4,5},{5,4},{6,7},{7,6},{8,9},{9,8},{10,11... | collective-permute-start | bytes 2949128 | tf_op jit(solution)/shard_map/ppermute | solution.py:388
  71.9 7.2 %collective-permute-start.6 = (bf16[8,96,128]{2,1,0:T(8,128)(2,1)}, bf16[8,96,128]{2,1,0:T(8,128)(2,1)S(1)}, u32[]{:S(2)}, u32[]{:S(2)}) collective-permute-start(bf16[8,96,128]{2,1,0:T(8,128)(2,1)} %get-tuple-element.22), channel_id=1, source_target_pairs={{1,32},{33,64},{65,96},{97,128},{129,160},{161,192},{193,224},{32,... | collective-permute-start | bytes 589832 | tf_op jit(solution)/shard_map/ppermute | solution.py:391
  79.1 0.7 copy-start.4
  79.1 1.0 copy-start.1
  80.1 11.6 %copy-start.3 = (bf16[32,96,128]{2,1,0:T(8,128)(2,1)S(1)}, bf16[32,96,128]{2,1,0:T(8,128)(2,1)}, u32[]{:S(2)}) copy-start(bf16[32,96,128]{2,1,0:T(8,128)(2,1)} %get-tuple-element.24) | copy-start | bytes 2359300
  85.1 8.7 %collective-permute-start.8 = (bf16[384,256]{1,0:T(8,128)(2,1)}, bf16[384,256]{1,0:T(8,128)(2,1)S(1)}, u32[]{:S(2)}, u32[]{:S(2)}) collective-permute-start(bf16[384,256]{1,0:T(8,128)(2,1)} %get-tuple-element.27), channel_id=1, source_target_pairs={{2,0},{4,2},{6,4},{8,6},{10,8},{12,10},{14,12},{16,14},{18,16},{20... | collective-permute-start | bytes 589832 | tf_op jit(solution)/shard_map/ppermute | solution.py:397
  87.0 8.7 %collective-permute-start.7 = (bf16[384,256]{1,0:T(8,128)(2,1)}, bf16[384,256]{1,0:T(8,128)(2,1)S(1)}, u32[]{:S(2)}, u32[]{:S(2)}) collective-permute-start(bf16[384,256]{1,0:T(8,128)(2,1)} %get-tuple-element.27), channel_id=1, source_target_pairs={{0,2},{2,4},{4,6},{6,8},{8,10},{10,12},{12,14},{14,16},{16,18},{18... | collective-permute-start | bytes 589832 | tf_op jit(solution)/shard_map/ppermute | solution.py:397
  93.8 2.0 %copy-start.6 = (bf16[384,256]{1,0:T(8,128)(2,1)}, bf16[384,256]{1,0:T(8,128)(2,1)S(1)}, u32[]{:S(2)}) copy-start(bf16[384,256]{1,0:T(8,128)(2,1)S(1)} %collective-permute-done.8.right_in) | copy-start | bytes 589828
  95.7 0.7 copy-start.7
  111.2 10.2 %collective-permute-start.9 = (bf16[8,192,128]{2,1,0:T(8,128)(2,1)}, bf16[8,192,128]{2,1,0:T(8,128)(2,1)S(1)}, u32[]{:S(2)}, u32[]{:S(2)}) collective-permute-start(bf16[8,192,128]{2,1,0:T(8,128)(2,1)} %get-tuple-element.29), channel_id=1, source_target_pairs={{0,1},{1,0},{2,3},{3,2},{4,5},{5,4},{6,7},{7,6},{8,9},{9,8},{10,11... | collective-permute-start | bytes 1179656 | tf_op jit(solution)/shard_map/ppermute | solution.py:388

commit v3 on v2

--- a/solution.py
+++ b/solution.py
@@ -16,16 +16,29 @@
 LINES = 16
 
 
+def whole_block(shape):
+    return pl.BlockSpec(shape, lambda _: (0,) * len(shape))
+
+
 def call(body, outs, scratch=(), flops=0, moved=0, name=None, ins=None):
-    return pl.pallas_call(
-        body,
-        **({} if ins is None else {"grid": (1,), "in_specs": ins}),
-        out_shape=tuple(jax.ShapeDtypeStruct(shape, kind) for shape, kind in outs),
-        scratch_shapes=list(scratch),
-        compiler_params=pltpu.CompilerParams(vmem_limit_bytes=VMEM_LIMIT),
-        cost_estimate=pl.CostEstimate(flops=flops, bytes_accessed=moved, transcendentals=0),
-        name=name,
-    )
+    def run(*operands):
+        specs = [None] * len(operands) if ins is None else ins
+        return pl.pallas_call(
+            body,
+            grid=(1,),
+            in_specs=[
+                whole_block(operand.shape) if spec is None else spec
+                for operand, spec in zip(operands, specs)
+            ],
+            out_specs=tuple(whole_block(shape) for shape, _ in outs),
+            out_shape=tuple(jax.ShapeDtypeStruct(shape, kind) for shape, kind in outs),
+            scratch_shapes=list(scratch),
+            compiler_params=pltpu.CompilerParams(vmem_limit_bytes=VMEM_LIMIT),
+            cost_estimate=pl.CostEstimate(flops=flops, bytes_accessed=moved, transcendentals=0),
+            name=name,
+        )(*operands)
+
+    return run
 
 
 def lane_of(shape):
@@ -287,7 +300,7 @@
             quads[2 * down + 1, :, at] = parted[:, LANES:]
         return carry
 
-    lax.fori_loop(0, rows // 4, step, 0)
+    lax.fori_loop(0, rows // 4, step, 0, unroll=2)
     base = hidden + channels
     for slot, place in enumerate((half, 1 - half)):
         total = None
@@ -362,7 +375,7 @@
             out_sib[row] = jnp.where(half == 0, top, low)
         return carry
 
-    lax.fori_loop(0, rows // 4, step, 0)
+    lax.fori_loop(0, rows // 4, step, 0, unroll=2)
 
 
 def on_device(
@@ -404,7 +417,6 @@
     hid_one, hid_two = (expand_one.shape[1], expand_two.shape[1])
     first_rows = hid_one + 5 * channels
     total_rows = first_rows + coarse_group + 2 * hid_two + coarse + group
-    own, reduce_one = lax.optimization_barrier((own, reduce_one))
     (packed_own,) = call(
         weights_body,
         [((total_rows, coarse), BF16)],
@@ -421,6 +433,7 @@
         kbias_one, ebias_one, pool_bias, kbias_two, ebias_two, gain_one, shift_one, rbias_one,
         scale_one, pool_gain, pool_shift, gain_two, shift_two, rbias_two, scale_two,
     )
+    packed_own, sib = lax.optimization_barrier((packed_own, sib))
     packed_sib = to_sibling(packed_own)
 
     def block(rows, start):
@@ -429,7 +442,6 @@
     taps_two_spec = block(coarse_group, first_rows)
     columns_spec = block(coarse, total_rows - group - coarse)
     taps_one_spec = block(group, total_rows - group)
-    full = pl.BlockSpec(memory_space=pltpu.VMEM)
     there = pl.BlockSpec(memory_space=pl.ANY)
 
     edge = [lax.dynamic_slice_in_dim(x, half_rows * half, SIDE, 0) for x in (own, sib)]
@@ -469,7 +481,7 @@
         flops=10**10,
         moved=10**7,
         name="section_one",
-        ins=[full] * 3 + [taps_one_spec] * 2 + [columns_spec] * 2 + [there] * 2,
+        ins=[None] * 3 + [taps_one_spec] * 2 + [columns_spec] * 2 + [there] * 2,
     )(whole, left_in, right_in, *[packed_own, packed_sib] * 3)
     from_sib = to_sibling(for_sib)
     from_outer = to_outer(for_outer)
@@ -479,7 +491,11 @@
         assemble_two_body,
         [((packed_rows + 2 * SIDE, coarse, LANES), BF16), side_shape],
         name="assemble_two",
-        ins=[full, pl.BlockSpec((message_rows, group, LANES), lambda _: (half_rows // message_rows, 0, 0)), full],
+        ins=[
+            None,
+            pl.BlockSpec((message_rows, group, LANES), lambda _: (half_rows // message_rows, 0, 0)),
+            None,
+        ],
     )(pooled, from_sib, from_outer)
     left_in, right_in = sides(own_sides)
     block_one = in_order(block_own, block_came).reshape(rows, group, cols).transpose(1, 0, 2)
@@ -493,7 +509,7 @@
         flops=10**10,
         moved=10**7,
         name="section_two",
-        ins=[full] * 3 + [taps_two_spec] * 2 + [columns_spec] * 2 + [there] * 2,
+        ins=[None] * 3 + [taps_two_spec] * 2 + [columns_spec] * 2 + [there] * 2,
     )(whole_two, left_in, right_in, *[packed_own, packed_sib] * 3)
     two_came = to_sibling(two_block_sib)
 

time: 123 us -> 118 us (0.959)
  waiting for transfers between devices: 22.2 us -> 15.4 us
  local copies, waits for them, and re-layouts: 11.3 us -> 13.4 us
  Pallas kernels: 51.9 us -> 50.5 us
    ppermute x4, waiting for transfers between devices: 5.89 us -> 0.36 us  [to_sibling(): return lax.ppermute(x, 'chan', swap)]
    pallas_call x5, Pallas kernels: 51.9 us -> 50.5 us  [run(): pl.pallas_call(body, grid=(1,), in_specs=[whole_block(operand.shape) if s...]
    ppermute x2, waiting for transfers between devices: 8.59 us -> 7.33 us  [to_outer(): return lax.ppermute(x, ('row', 'chan'), outward)]
    another operation x1 -> x2, local copies, waits for them, and re-layouts: 2.67 us -> 3.86 us
    unnamed x22 -> x21, local copies, waits for them, and re-layouts: 3.21 us -> 4.11 us
  transfers between devices with their start and end apart: 10 -> 10, of which waited for: 6 -> 5; matrix products, arithmetic and copies ran while one was open for 4% -> 6% of each run, Pallas kernels for 3% -> 7%
where the time goes in v3:
time: 118 us; the launch traced here: 117 us
  Pallas kernels  50.5 us (43%)
  starting transfers between devices  36.7 us (31%)
  waiting for transfers between devices  15.4 us (13%)
  local copies, waits for them, and re-layouts  13.4 us (11%)
    pallas_call x5, Pallas kernels, run(): pl.pallas_call(body, grid=(1,), in_specs=[whole_block(operand.shape) if s...  50.5 us
    ppermute x4, starting transfers between devices, to_sibling(): return lax.ppermute(x, 'chan', swap)  19 us
    ppermute x2, waiting for transfers between devices, sides(): lax.ppermute(own_sides, 'col', right)  7.69 us
    ppermute x2, waiting for transfers between devices, to_outer(): return lax.ppermute(x, ('row', 'chan'), outward)  7.33 us
    ppermute x2, starting transfers between devices, sides(): lax.ppermute(own_sides, 'col', left)  6.98 us
    ppermute x2, starting transfers between devices, sides(): lax.ppermute(own_sides, 'col', right)  5.46 us
    ppermute x2, starting transfers between devices, to_outer(): return lax.ppermute(x, ('row', 'chan'), outward)  5.27 us
    unnamed x21, local copies, waits for them, and re-layouts  4.11 us
  transfers between devices with their start and end apart: 10, of which 5 were waited for; matrix products, arithmetic and copies ran while one was open for 6% of the time, Pallas kernels for 7%

profile of v3, /device:TPU:225, one launch (start us, length us, event | category | flops | bytes accessed | tf_op | source)
XLA Modules:
  0.0 117.4 jit_solution(13132523440044251098)
XLA Ops:
  0.6 2.7 %constant_dynamic-slice_fusion.2 = (bf16[96,35,128]{2,1,0:T(8,128)(2,1)S(1)}, bf16[96,35,128]{2,1,0:T(8,128)(2,1)S(1)}) fusion(bf16[96,64,128]{2,1,0:T(8,128)(2,1)} %param.23, s32[]{:T(128)S(6)} %select_n.36, s32[]{:T(128)S(6)} %select_n.35), kind=kLoop, calls=%fused_computation.11 | loop fusion | bytes 3440648 | tf_op jit(solution)/shard_map/dynamic-slice.1
  3.3 0.1 copy.51
  3.4 0.8 collective-permute-start
  4.2 3.8 %turn_weights.1.taps_own.columns_own.packed_own = bf16[3552,384]{1,0:T(8,128)(2,1)} custom-call(bf16[192,384]{1,0:T(8,128)(2,1)} %expand_one.1, bf16[192,384]{1,0:T(8,128)(2,1)} %bitcast.33, bf16[4,192,192]{2,1,0:T(8,128)(2,1)} %pool.1, bf16[384,768]{1,0:T(8,128)(2,1)} %expand_two.1, bf16[768,384]{1,0:T(8,128)(2,1)} %reduce_two.1, f32[7,7,96]{2,1,0:T(8,128)} %bitcast.35, ...), custom_call_target="tpu_custom_call" | custom-call | bytes 10000000 | tf_op jit(solution)/shard_map/turn_weights/pallas_call | solution.py:26
  8.0 0.0 collective-permute-done.sib
  8.0 0.0 copy-start.1
  8.0 0.1 collective-permute-start.4
  8.2 1.2 %constant_dynamic-slice_fusion.1 = bf16[96,3,128]{2,1,0:T(4,128)(2,1)S(1)} fusion(bf16[96,64,128]{2,1,0:T(8,128)(2,1)} %param.23, s32[]{:T(128)S(6)} %add.18), kind=kLoop, calls=%fused_computation.10 | loop fusion | bytes 147460 | tf_op jit(solution)/shard_map/dynamic-slice.2
  9.4 3.4 %collective-permute-start.1 = (bf16[3,192,128]{2,1,0:T(8,128)(2,1)S(1)}, bf16[3,192,128]{2,1,0:T(8,128)(2,1)S(1)}, u32[]{:S(2)}, u32[]{:S(2)}) collective-permute-start(bf16[3,192,128]{2,1,0:T(8,128)(2,1)S(1)} %pad_maximum_fusion), channel_id=1, source_target_pairs={{1,32},{33,64},{65,96},{97,128},{129,160},{161,192},{193,224},{32,... | collective-permute-start | bytes 442376 | tf_op jit(solution)/shard_map/ppermute | solution.py:404
  12.8 1.0 copy.52
  13.8 2.1 %collective-permute-done.1.outer = bf16[3,192,128]{2,1,0:T(8,128)(2,1)S(1)} collective-permute-done((bf16[3,192,128]{2,1,0:T(8,128)(2,1)S(1)}, bf16[3,192,128]{2,1,0:T(8,128)(2,1)S(1)}, u32[]{:S(2)}, u32[]{:S(2)}) %collective-permute-start.1) | collective-permute-done | bytes 147488 | tf_op jit(solution)/shard_map/ppermute | solution.py:404
  15.9 0.0 copy-start.4
  15.9 0.0 copy-done.1
  15.9 0.6 copy-done.4
  16.5 4.1 %assemble_one.1 = (bf16[38,192,128]{2,1,0:T(8,128)(2,1)}, bf16[192,256]{1,0:T(8,128)(2,1)}) custom-call(bf16[35,96,128]{2,1,0:T(8,128)(2,1)} %bitcast.25, bf16[35,96,128]{2,1,0:T(8,128)(2,1)} %copy-done.1, bf16[3,192,128]{2,1,0:T(8,128)(2,1)} %copy-done.4), custom_call_target="tpu_custom_call" | custom-call | tf_op jit(solution)/shard_map/assemble_one/pallas_call | solution.py:26
  20.7 5.1 %collective-permute-start.3 = (bf16[192,256]{1,0:T(8,128)(2,1)}, bf16[192,256]{1,0:T(8,128)(2,1)S(1)}, u32[]{:S(2)}, u32[]{:S(2)}) collective-permute-start(bf16[192,256]{1,0:T(8,128)(2,1)} %get-tuple-element.18), channel_id=1, source_target_pairs={{2,0},{4,2},{6,4},{8,6},{10,8},{12,10},{14,12},{16,14},{18,16},{20... | collective-permute-start | bytes 294920 | tf_op jit(solution)/shard_map/ppermute | solution.py:410
  25.8 1.9 %collective-permute-start.2 = (bf16[192,256]{1,0:T(8,128)(2,1)}, bf16[192,256]{1,0:T(8,128)(2,1)S(1)}, u32[]{:S(2)}, u32[]{:S(2)}) collective-permute-start(bf16[192,256]{1,0:T(8,128)(2,1)} %get-tuple-element.18), channel_id=1, source_target_pairs={{0,2},{2,4},{4,6},{6,8},{8,10},{10,12},{12,14},{14,16},{16,18},{18... | collective-permute-start | bytes 294920 | tf_op jit(solution)/shard_map/ppermute | solution.py:410
  27.7 0.0 collective-permute-done.3.right_in
  27.7 0.0 copy-start.7
  27.7 5.7 %collective-permute-done.2.left_in = bf16[192,256]{1,0:T(8,128)(2,1)S(1)} collective-permute-done((bf16[192,256]{1,0:T(8,128)(2,1)}, bf16[192,256]{1,0:T(8,128)(2,1)S(1)}, u32[]{:S(2)}, u32[]{:S(2)}) %collective-permute-start.2) | collective-permute-done | bytes 98336 | tf_op jit(solution)/shard_map/ppermute | solution.py:410
  33.4 0.0 collective-permute-done.4.taps_sib.columns_sib.packed_sib
  33.5 0.0 copy-done.7
  33.5 0.6 copy-done.8
  34.1 23.1 %section_one.1 = (bf16[32,96,128]{2,1,0:T(8,128)(2,1)}, bf16[40,96,128]{2,1,0:T(8,128)(2,1)}, bf16[8,384,128]{2,1,0:T(8,128)(2,1)}, bf16[8,96,128]{2,1,0:T(8,128)(2,1)}) custom-call(bf16[38,192,128]{2,1,0:T(8,128)(2,1)} %get-tuple-element.17.whole, bf16[192,256]{1,0:T(8,128)(2,1)} %copy-done.8, bf16[192,256]{1,0:T(8,128)(2,1)} %copy-done.7, ...), custom_call_target="tpu_custom_call" | custom-call | flops 10000000000 | bytes 10000000 | tf_op jit(solution)/shard_map/section_one/pallas_call | solution.py:26
  57.2 9.5 %collective-permute-start.5 = (bf16[40,96,128]{2,1,0:T(8,128)(2,1)}, bf16[40,96,128]{2,1,0:T(8,128)(2,1)S(1)}, u32[]{:S(2)}, u32[]{:S(2)}) collective-permute-start(bf16[40,96,128]{2,1,0:T(8,128)(2,1)} %get-tuple-element.21), channel_id=1, source_target_pairs={{0,1},{1,0},{2,3},{3,2},{4,5},{5,4},{6,7},{7,6},{8,9},{9,8},{10,11... | collective-permute-start | bytes 2949128 | tf_op jit(solution)/shard_map/ppermute | solution.py:401
  66.7 1.9 %collective-permute-start.6 = (bf16[8,96,128]{2,1,0:T(8,128)(2,1)}, bf16[8,96,128]{2,1,0:T(8,128)(2,1)S(1)}, u32[]{:S(2)}, u32[]{:S(2)}) collective-permute-start(bf16[8,96,128]{2,1,0:T(8,128)(2,1)} %get-tuple-element.22), channel_id=1, source_target_pairs={{1,32},{33,64},{65,96},{97,128},{129,160},{161,192},{193,224},{32,... | collective-permute-start | bytes 589832 | tf_op jit(solution)/shard_map/ppermute | solution.py:404
  68.6 5.3 %collective-permute-done.6.from_outer = bf16[8,96,128]{2,1,0:T(8,128)(2,1)S(1)} collective-permute-done((bf16[8,96,128]{2,1,0:T(8,128)(2,1)}, bf16[8,96,128]{2,1,0:T(8,128)(2,1)S(1)}, u32[]{:S(2)}, u32[]{:S(2)}) %collective-permute-start.6) | collective-permute-done | bytes 196640 | tf_op jit(solution)/shard_map/ppermute | solution.py:404
  73.9 0.0 collective-permute-done.5.from_sib
  73.9 0.7 copy-done.3
  74.5 0.3 copy-done
  74.9 5.0 %assemble_two.1 = (bf16[14,384,128]{2,1,0:T(8,128)(2,1)}, bf16[384,256]{1,0:T(8,128)(2,1)}) custom-call(bf16[8,384,128]{2,1,0:T(8,128)(2,1)} %get-tuple-element.20.pooled, bf16[40,96,128]{2,1,0:T(8,128)(2,1)} %copy-done, bf16[8,96,128]{2,1,0:T(8,128)(2,1)} %copy-done.3), custom_call_target="tpu_custom_call" | custom-call | tf_op jit(solution)/shard_map/assemble_two/pallas_call | solution.py:26
  79.8 1.9 %collective-permute-start.8 = (bf16[384,256]{1,0:T(8,128)(2,1)}, bf16[384,256]{1,0:T(8,128)(2,1)S(1)}, u32[]{:S(2)}, u32[]{:S(2)}) collective-permute-start(bf16[384,256]{1,0:T(8,128)(2,1)} %get-tuple-element.27), channel_id=1, source_target_pairs={{2,0},{4,2},{6,4},{8,6},{10,8},{12,10},{14,12},{16,14},{18,16},{20... | collective-permute-start | bytes 589832 | tf_op jit(solution)/shard_map/ppermute | solution.py:410
  81.7 3.5 %collective-permute-start.7 = (bf16[384,256]{1,0:T(8,128)(2,1)}, bf16[384,256]{1,0:T(8,128)(2,1)S(1)}, u32[]{:S(2)}, u32[]{:S(2)}) collective-permute-start(bf16[384,256]{1,0:T(8,128)(2,1)} %get-tuple-element.27), channel_id=1, source_target_pairs={{0,2},{2,4},{4,6},{6,8},{8,10},{10,12},{12,14},{14,16},{16,18},{18... | collective-permute-start | bytes 589832 | tf_op jit(solution)/shard_map/ppermute | solution.py:410
  85.3 1.2 %slice_bitcast_fusion = bf16[1,32,96,128]{3,2,1,0:T(8,128)(2,1)S(1)} fusion(bf16[40,96,128]{2,1,0:T(8,128)(2,1)} %copy-done), kind=kLoop, calls=%fused_computation.6 | loop fusion | bytes 1572864 | tf_op jit(solution)/shard_map/stack | solution.py:407
  86.5 0.0 copy-done.2
  86.5 0.3 maximum_select_fusion
  86.8 1.8 %copy.50 = bf16[64,96,128]{2,0,1:T(8,128)(2,1)} copy(bf16[64,96,128]{2,1,0:T(8,128)(2,1)S(1)} %bitcast.24) | data formatting | bytes 3145728 | tf_op jit(solution)/shard_map/jit(_where)/select_n | solution.py:407
  88.5 0.0 collective-permute-done.8.right_in
  88.5 2.0 %collective-permute-done.7.left_in = bf16[384,256]{1,0:T(8,128)(2,1)S(1)} collective-permute-done((bf16[384,256]{1,0:T(8,128)(2,1)}, bf16[384,256]{1,0:T(8,128)(2,1)S(1)}, u32[]{:S(2)}, u32[]{:S(2)}) %collective-permute-start.7) | collective-permute-done | bytes 196640 | tf_op jit(solution)/shard_map/ppermute | solution.py:410
  90.5 0.0 copy-done.5
  90.5 0.7 copy-done.6
  91.2 14.5 %section_two.1 = (bf16[8,192,128]{2,1,0:T(8,128)(2,1)}, bf16[8,192,128]{2,1,0:T(8,128)(2,1)}) custom-call(bf16[14,384,128]{2,1,0:T(8,128)(2,1)} %get-tuple-element.26.whole, bf16[384,256]{1,0:T(8,128)(2,1)} %copy-done.6, bf16[384,256]{1,0:T(8,128)(2,1)} %copy-done.5, bf16[3552,384]{1,0:T(8,128)(2,1)} %turn_weights.1.taps_own.columns_own.packed_own, ...), custom_call_target="tpu_custom_call" | custom-call | flops 10000000000 | bytes 10000000 | tf_op jit(solution)/shard_map/section_two/pallas_call | solution.py:26
  105.7 8.6 %collective-permute-start.9 = (bf16[8,192,128]{2,1,0:T(8,128)(2,1)}, bf16[8,192,128]{2,1,0:T(8,128)(2,1)S(1)}, u32[]{:S(2)}, u32[]{:S(2)}) collective-permute-start(bf16[8,192,128]{2,1,0:T(8,128)(2,1)} %get-tuple-element.29), channel_id=1, source_target_pairs={{0,1},{1,0},{2,3},{3,2},{4,5},{5,4},{6,7},{7,6},{8,9},{9,8},{10,11... | collective-permute-start | bytes 1179656 | tf_op jit(solution)/shard_map/ppermute | solution.py:401
  114.3 1.2 %copy.40 = bf16[8,192,128]{1,2,0:T(8,128)(2,1)S(1)} copy(bf16[8,192,128]{2,1,0:T(8,128)(2,1)} %get-tuple-element.28) | data formatting | bytes 786432 | tf_op jit(solution)/shard_map/section_two/pallas_call | solution.py:26
  115.5 0.4 collective-permute-done.9
  115.8 0.2 copy.41
  116.0 0.3 fusion
  116.4 1.0 copy.42
  (9 shorter events, 0.1 us)
Async XLA Ops:
  3.4 4.6 %collective-permute-start = (bf16[35,96,128]{2,1,0:T(8,128)(2,1)S(1)}, bf16[35,96,128]{2,1,0:T(8,128)(2,1)S(1)}, u32[]{:S(2)}, u32[]{:S(2)}) collective-permute-start(bf16[35,96,128]{2,1,0:T(8,128)(2,1)S(1)} %bitcast.30), channel_id=1, source_target_pairs={{0,1},{1,0},{2,3},{3,2},{4,5},{5,4},{6,7},{7,6},{8,9},{9,8},{10,11... | collective-permute-start | bytes 2580488 | tf_op jit(solution)/shard_map/ppermute | solution.py:401
  8.0 7.9 %copy-start.1 = (bf16[35,96,128]{2,1,0:T(8,128)(2,1)}, bf16[35,96,128]{2,1,0:T(8,128)(2,1)S(1)}, u32[]{:S(2)}) copy-start(bf16[35,96,128]{2,1,0:T(8,128)(2,1)S(1)} %collective-permute-done.sib) | copy-start | bytes 2580484
  8.0 25.4 %collective-permute-start.4 = (bf16[3552,384]{1,0:T(8,128)(2,1)}, bf16[3552,384]{1,0:T(8,128)(2,1)}, u32[]{:S(2)}, u32[]{:S(2)}) collective-permute-start(bf16[3552,384]{1,0:T(8,128)(2,1)} %turn_weights.1.taps_own.columns_own.packed_own), channel_id=1, source_target_pairs={{0,1},{1,0},{2,3},{3,2},{4,5},{5,4},{6,7},{7,6},{8,9},{9,8},{10,11... | collective-permute-start | bytes 8183816 | tf_op jit(solution)/shard_map/ppermute | solution.py:401
  9.4 6.5 %collective-permute-start.1 = (bf16[3,192,128]{2,1,0:T(8,128)(2,1)S(1)}, bf16[3,192,128]{2,1,0:T(8,128)(2,1)S(1)}, u32[]{:S(2)}, u32[]{:S(2)}) collective-permute-start(bf16[3,192,128]{2,1,0:T(8,128)(2,1)S(1)} %pad_maximum_fusion), channel_id=1, source_target_pairs={{1,32},{33,64},{65,96},{97,128},{129,160},{161,192},{193,224},{32,... | collective-permute-start | bytes 442376 | tf_op jit(solution)/shard_map/ppermute | solution.py:404
  15.9 0.6 copy-start.4
  20.7 7.0 %collective-permute-start.3 = (bf16[192,256]{1,0:T(8,128)(2,1)}, bf16[192,256]{1,0:T(8,128)(2,1)S(1)}, u32[]{:S(2)}, u32[]{:S(2)}) collective-permute-start(bf16[192,256]{1,0:T(8,128)(2,1)} %get-tuple-element.18), channel_id=1, source_target_pairs={{2,0},{4,2},{6,4},{8,6},{10,8},{12,10},{14,12},{16,14},{18,16},{20... | collective-permute-start | bytes 294920 | tf_op jit(solution)/shard_map/ppermute | solution.py:410
  25.8 7.7 %collective-permute-start.2 = (bf16[192,256]{1,0:T(8,128)(2,1)}, bf16[192,256]{1,0:T(8,128)(2,1)S(1)}, u32[]{:S(2)}, u32[]{:S(2)}) collective-permute-start(bf16[192,256]{1,0:T(8,128)(2,1)} %get-tuple-element.18), channel_id=1, source_target_pairs={{0,2},{2,4},{4,6},{6,8},{8,10},{10,12},{12,14},{14,16},{16,18},{18... | collective-permute-start | bytes 294920 | tf_op jit(solution)/shard_map/ppermute | solution.py:410
  27.7 5.8 %copy-start.7 = (bf16[192,256]{1,0:T(8,128)(2,1)}, bf16[192,256]{1,0:T(8,128)(2,1)S(1)}, u32[]{:S(2)}) copy-start(bf16[192,256]{1,0:T(8,128)(2,1)S(1)} %collective-permute-done.3.right_in) | copy-start | bytes 294916
  33.4 0.6 copy-start.8
  57.2 16.7 %collective-permute-start.5 = (bf16[40,96,128]{2,1,0:T(8,128)(2,1)}, bf16[40,96,128]{2,1,0:T(8,128)(2,1)S(1)}, u32[]{:S(2)}, u32[]{:S(2)}) collective-permute-start(bf16[40,96,128]{2,1,0:T(8,128)(2,1)} %get-tuple-element.21), channel_id=1, source_target_pairs={{0,1},{1,0},{2,3},{3,2},{4,5},{5,4},{6,7},{7,6},{8,9},{9,8},{10,11... | collective-permute-start | bytes 2949128 | tf_op jit(solution)/shard_map/ppermute | solution.py:401
  66.7 7.2 %collective-permute-start.6 = (bf16[8,96,128]{2,1,0:T(8,128)(2,1)}, bf16[8,96,128]{2,1,0:T(8,128)(2,1)S(1)}, u32[]{:S(2)}, u32[]{:S(2)}) collective-permute-start(bf16[8,96,128]{2,1,0:T(8,128)(2,1)} %get-tuple-element.22), channel_id=1, source_target_pairs={{1,32},{33,64},{65,96},{97,128},{129,160},{161,192},{193,224},{32,... | collective-permute-start | bytes 589832 | tf_op jit(solution)/shard_map/ppermute | solution.py:404
  73.9 0.7 copy-start.3
  73.9 1.0 copy-start
  74.9 11.6 %copy-start.2 = (bf16[32,96,128]{2,1,0:T(8,128)(2,1)S(1)}, bf16[32,96,128]{2,1,0:T(8,128)(2,1)}, u32[]{:S(2)}) copy-start(bf16[32,96,128]{2,1,0:T(8,128)(2,1)} %get-tuple-element.24) | copy-start | bytes 2359300
  79.8 8.7 %collective-permute-start.8 = (bf16[384,256]{1,0:T(8,128)(2,1)}, bf16[384,256]{1,0:T(8,128)(2,1)S(1)}, u32[]{:S(2)}, u32[]{:S(2)}) collective-permute-start(bf16[384,256]{1,0:T(8,128)(2,1)} %get-tuple-element.27), channel_id=1, source_target_pairs={{2,0},{4,2},{6,4},{8,6},{10,8},{12,10},{14,12},{16,14},{18,16},{20... | collective-permute-start | bytes 589832 | tf_op jit(solution)/shard_map/ppermute | solution.py:410
  81.7 8.7 %collective-permute-start.7 = (bf16[384,256]{1,0:T(8,128)(2,1)}, bf16[384,256]{1,0:T(8,128)(2,1)S(1)}, u32[]{:S(2)}, u32[]{:S(2)}) collective-permute-start(bf16[384,256]{1,0:T(8,128)(2,1)} %get-tuple-element.27), channel_id=1, source_target_pairs={{0,2},{2,4},{4,6},{6,8},{8,10},{10,12},{12,14},{14,16},{16,18},{18... | collective-permute-start | bytes 589832 | tf_op jit(solution)/shard_map/ppermute | solution.py:410
  88.5 2.0 %copy-start.5 = (bf16[384,256]{1,0:T(8,128)(2,1)}, bf16[384,256]{1,0:T(8,128)(2,1)S(1)}, u32[]{:S(2)}) copy-start(bf16[384,256]{1,0:T(8,128)(2,1)S(1)} %collective-permute-done.8.right_in) | copy-start | bytes 589828
  90.5 0.7 copy-start.6
  105.7 10.2 %collective-permute-start.9 = (bf16[8,192,128]{2,1,0:T(8,128)(2,1)}, bf16[8,192,128]{2,1,0:T(8,128)(2,1)S(1)}, u32[]{:S(2)}, u32[]{:S(2)}) collective-permute-start(bf16[8,192,128]{2,1,0:T(8,128)(2,1)} %get-tuple-element.29), channel_id=1, source_target_pairs={{0,1},{1,0},{2,3},{3,2},{4,5},{5,4},{6,7},{7,6},{8,9},{9,8},{10,11... | collective-permute-start | bytes 1179656 | tf_op jit(solution)/shard_map/ppermute | solution.py:401

commit v4 on v3

--- a/solution.py
+++ b/solution.py
@@ -411,7 +411,6 @@
 
     turned = image.transpose(1, 0, 2)
     span = half_rows + SIDE
-    own = lax.dynamic_slice_in_dim(turned, (half_rows - SIDE) * half, span, 0)
     sib = to_sibling(lax.dynamic_slice_in_dim(turned, (half_rows - SIDE) * (1 - half), span, 0))
 
     hid_one, hid_two = (expand_one.shape[1], expand_two.shape[1])
@@ -433,7 +432,9 @@
         kbias_one, ebias_one, pool_bias, kbias_two, ebias_two, gain_one, shift_one, rbias_one,
         scale_one, pool_gain, pool_shift, gain_two, shift_two, rbias_two, scale_two,
     )
-    packed_own, sib = lax.optimization_barrier((packed_own, sib))
+    packed_own, sib, image = lax.optimization_barrier((packed_own, sib, image))
+    own_at = (half_rows - SIDE) * half
+    own = lax.dynamic_slice_in_dim(image, own_at, span, 1).transpose(1, 0, 2)
     packed_sib = to_sibling(packed_own)
 
     def block(rows, start):
@@ -444,7 +445,10 @@
     taps_one_spec = block(group, total_rows - group)
     there = pl.BlockSpec(memory_space=pl.ANY)
 
-    edge = [lax.dynamic_slice_in_dim(x, half_rows * half, SIDE, 0) for x in (own, sib)]
+    edge = [
+        lax.dynamic_slice_in_dim(image, (rows - SIDE) * half, SIDE, 1).transpose(1, 0, 2),
+        lax.dynamic_slice_in_dim(sib, half_rows * half, SIDE, 0),
+    ]
     outer = to_outer(jnp.concatenate(edge, axis=1))
     side_shape = ((channels, 2 * LANES), BF16)
     whole, own_sides = call(

time: 118 us -> 118 us (level)
    another operation x2 -> x1, local copies, waits for them, and re-layouts: 3.86 us -> 1.73 us
    unnamed x21 -> x19, local copies, waits for them, and re-layouts: 4.11 us -> 3.09 us
where the time goes in v4:
time: 118 us; the launch traced here: 117 us
  Pallas kernels  50.6 us (43%)
  starting transfers between devices  36.9 us (31%)
  waiting for transfers between devices  15.3 us (13%)
  local copies, waits for them, and re-layouts  13.1 us (11%)
    pallas_call x5, Pallas kernels, run(): pl.pallas_call(body, grid=(1,), in_specs=[whole_block(operand.shape) if s...  50.6 us
    ppermute x4, starting transfers between devices, to_sibling(): return lax.ppermute(x, 'chan', swap)  19 us
    ppermute x2, waiting for transfers between devices, sides(): lax.ppermute(own_sides, 'col', right)  7.69 us
    ppermute x2, waiting for transfers between devices, to_outer(): return lax.ppermute(x, ('row', 'chan'), outward)  7.28 us
    ppermute x2, starting transfers between devices, sides(): lax.ppermute(own_sides, 'col', left)  6.98 us
    ppermute x2, starting transfers between devices, sides(): lax.ppermute(own_sides, 'col', right)  5.46 us
    ppermute x2, starting transfers between devices, to_outer(): return lax.ppermute(x, ('row', 'chan'), outward)  5.38 us
    unnamed x19, local copies, waits for them, and re-layouts  3.09 us
  transfers between devices with their start and end apart: 10, of which 5 were waited for; matrix products, arithmetic and copies ran while one was open for 6% of the time, Pallas kernels for 7%

profile of v4, /device:TPU:225, one launch (start us, length us, event | category | flops | bytes accessed | tf_op | source)
XLA Modules:
  0.0 117.4 jit_solution(16769003323726408595)
XLA Ops:
  0.6 1.7 %constant_dynamic-slice_fusion.1 = bf16[96,35,128]{2,1,0:T(8,128)(2,1)S(1)} fusion(bf16[96,64,128]{2,1,0:T(8,128)(2,1)} %param.23, s32[]{:T(128)S(6)} %select_n.33), kind=kLoop, calls=%fused_computation.10 | loop fusion | bytes 1720324 | tf_op jit(solution)/shard_map/dynamic-slice
  2.4 0.1 copy.47
  2.5 0.7 collective-permute-start
  3.2 0.0 copy-start
  3.2 3.9 %turn_weights.1.taps_own.columns_own.packed_own = bf16[3552,384]{1,0:T(8,128)(2,1)} custom-call(bf16[192,384]{1,0:T(8,128)(2,1)} %expand_one.1, bf16[192,384]{1,0:T(8,128)(2,1)} %bitcast.29, bf16[4,192,192]{2,1,0:T(8,128)(2,1)} %pool.1, bf16[384,768]{1,0:T(8,128)(2,1)} %expand_two.1, bf16[768,384]{1,0:T(8,128)(2,1)} %reduce_two.1, f32[7,7,96]{2,1,0:T(8,128)} %bitcast.31, ...), custom_call_target="tpu_custom_call" | custom-call | bytes 10000000 | tf_op jit(solution)/shard_map/turn_weights/pallas_call | solution.py:26
  7.1 0.0 collective-permute-done.sib
  7.1 0.1 collective-permute-start.4
  7.3 0.0 copy-done
  7.3 1.0 copy.37
  8.3 0.9 constant_dynamic-slice_fusion
  9.2 3.5 %collective-permute-start.1 = (bf16[3,192,128]{2,1,0:T(8,128)(2,1)S(1)}, bf16[3,192,128]{2,1,0:T(8,128)(2,1)S(1)}, u32[]{:S(2)}, u32[]{:S(2)}) collective-permute-start(bf16[3,192,128]{2,1,0:T(8,128)(2,1)S(1)} %pad_maximum_fusion), channel_id=1, source_target_pairs={{1,32},{33,64},{65,96},{97,128},{129,160},{161,192},{193,224},{32,... | collective-permute-start | bytes 442376 | tf_op jit(solution)/shard_map/ppermute | solution.py:404
  12.7 1.0 dynamic-slice_bitcast_fusion.own
  13.7 2.0 %collective-permute-done.1.outer = bf16[3,192,128]{2,1,0:T(8,128)(2,1)S(1)} collective-permute-done((bf16[3,192,128]{2,1,0:T(8,128)(2,1)S(1)}, bf16[3,192,128]{2,1,0:T(8,128)(2,1)S(1)}, u32[]{:S(2)}, u32[]{:S(2)}) %collective-permute-start.1) | collective-permute-done | bytes 147488 | tf_op jit(solution)/shard_map/ppermute | solution.py:404
  15.7 0.7 copy-done.4
  16.3 4.1 %assemble_one.1 = (bf16[38,192,128]{2,1,0:T(8,128)(2,1)}, bf16[192,256]{1,0:T(8,128)(2,1)}) custom-call(bf16[35,96,128]{2,1,0:T(8,128)(2,1)} %dynamic-slice_bitcast_fusion.own, bf16[35,96,128]{2,1,0:T(8,128)(2,1)} %collective-permute-done.sib, bf16[3,192,128]{2,1,0:T(8,128)(2,1)} %copy-done.4), custom_call_target="tpu_custom_call" | custom-call | tf_op jit(solution)/shard_map/assemble_one/pallas_call | solution.py:26
  20.5 5.1 %collective-permute-start.3 = (bf16[192,256]{1,0:T(8,128)(2,1)}, bf16[192,256]{1,0:T(8,128)(2,1)S(1)}, u32[]{:S(2)}, u32[]{:S(2)}) collective-permute-start(bf16[192,256]{1,0:T(8,128)(2,1)} %get-tuple-element.20), channel_id=1, source_target_pairs={{2,0},{4,2},{6,4},{8,6},{10,8},{12,10},{14,12},{16,14},{18,16},{20... | collective-permute-start | bytes 294920 | tf_op jit(solution)/shard_map/ppermute | solution.py:410
  25.6 1.9 %collective-permute-start.2 = (bf16[192,256]{1,0:T(8,128)(2,1)}, bf16[192,256]{1,0:T(8,128)(2,1)S(1)}, u32[]{:S(2)}, u32[]{:S(2)}) collective-permute-start(bf16[192,256]{1,0:T(8,128)(2,1)} %get-tuple-element.20), channel_id=1, source_target_pairs={{0,2},{2,4},{4,6},{6,8},{8,10},{10,12},{12,14},{14,16},{16,18},{18... | collective-permute-start | bytes 294920 | tf_op jit(solution)/shard_map/ppermute | solution.py:410
  27.5 0.0 collective-permute-done.3.right_in
  27.5 0.0 copy-start.7
  27.5 5.7 %collective-permute-done.2.left_in = bf16[192,256]{1,0:T(8,128)(2,1)S(1)} collective-permute-done((bf16[192,256]{1,0:T(8,128)(2,1)}, bf16[192,256]{1,0:T(8,128)(2,1)S(1)}, u32[]{:S(2)}, u32[]{:S(2)}) %collective-permute-start.2) | collective-permute-done | bytes 98336 | tf_op jit(solution)/shard_map/ppermute | solution.py:410
  33.3 0.0 collective-permute-done.4.taps_sib.columns_sib.packed_sib
  33.3 0.0 copy-done.7
  33.3 0.6 copy-done.8
  33.9 23.1 %section_one.1 = (bf16[32,96,128]{2,1,0:T(8,128)(2,1)}, bf16[40,96,128]{2,1,0:T(8,128)(2,1)}, bf16[8,384,128]{2,1,0:T(8,128)(2,1)}, bf16[8,96,128]{2,1,0:T(8,128)(2,1)}) custom-call(bf16[38,192,128]{2,1,0:T(8,128)(2,1)} %get-tuple-element.19.whole, bf16[192,256]{1,0:T(8,128)(2,1)} %copy-done.8, bf16[192,256]{1,0:T(8,128)(2,1)} %copy-done.7, ...), custom_call_target="tpu_custom_call" | custom-call | flops 10000000000 | bytes 10000000 | tf_op jit(solution)/shard_map/section_one/pallas_call | solution.py:26
  57.0 9.6 %collective-permute-start.5 = (bf16[40,96,128]{2,1,0:T(8,128)(2,1)}, bf16[40,96,128]{2,1,0:T(8,128)(2,1)S(1)}, u32[]{:S(2)}, u32[]{:S(2)}) collective-permute-start(bf16[40,96,128]{2,1,0:T(8,128)(2,1)} %get-tuple-element.23), channel_id=1, source_target_pairs={{0,1},{1,0},{2,3},{3,2},{4,5},{5,4},{6,7},{7,6},{8,9},{9,8},{10,11... | collective-permute-start | bytes 2949128 | tf_op jit(solution)/shard_map/ppermute | solution.py:401
  66.6 1.9 %collective-permute-start.6 = (bf16[8,96,128]{2,1,0:T(8,128)(2,1)}, bf16[8,96,128]{2,1,0:T(8,128)(2,1)S(1)}, u32[]{:S(2)}, u32[]{:S(2)}) collective-permute-start(bf16[8,96,128]{2,1,0:T(8,128)(2,1)} %get-tuple-element.24), channel_id=1, source_target_pairs={{1,32},{33,64},{65,96},{97,128},{129,160},{161,192},{193,224},{32,... | collective-permute-start | bytes 589832 | tf_op jit(solution)/shard_map/ppermute | solution.py:404
  68.5 5.3 %collective-permute-done.6.from_outer = bf16[8,96,128]{2,1,0:T(8,128)(2,1)S(1)} collective-permute-done((bf16[8,96,128]{2,1,0:T(8,128)(2,1)}, bf16[8,96,128]{2,1,0:T(8,128)(2,1)S(1)}, u32[]{:S(2)}, u32[]{:S(2)}) %collective-permute-start.6) | collective-permute-done | bytes 196640 | tf_op jit(solution)/shard_map/ppermute | solution.py:404
  73.8 0.0 collective-permute-done.5.from_sib
  73.8 0.7 copy-done.3
  74.5 0.3 copy-done.1
  74.8 5.0 %assemble_two.1 = (bf16[14,384,128]{2,1,0:T(8,128)(2,1)}, bf16[384,256]{1,0:T(8,128)(2,1)}) custom-call(bf16[8,384,128]{2,1,0:T(8,128)(2,1)} %get-tuple-element.22.pooled, bf16[40,96,128]{2,1,0:T(8,128)(2,1)} %copy-done.1, bf16[8,96,128]{2,1,0:T(8,128)(2,1)} %copy-done.3), custom_call_target="tpu_custom_call" | custom-call | tf_op jit(solution)/shard_map/assemble_two/pallas_call | solution.py:26
  79.8 1.9 %collective-permute-start.8 = (bf16[384,256]{1,0:T(8,128)(2,1)}, bf16[384,256]{1,0:T(8,128)(2,1)S(1)}, u32[]{:S(2)}, u32[]{:S(2)}) collective-permute-start(bf16[384,256]{1,0:T(8,128)(2,1)} %get-tuple-element.29), channel_id=1, source_target_pairs={{2,0},{4,2},{6,4},{8,6},{10,8},{12,10},{14,12},{16,14},{18,16},{20... | collective-permute-start | bytes 589832 | tf_op jit(solution)/shard_map/ppermute | solution.py:410
  81.7 3.5 %collective-permute-start.7 = (bf16[384,256]{1,0:T(8,128)(2,1)}, bf16[384,256]{1,0:T(8,128)(2,1)S(1)}, u32[]{:S(2)}, u32[]{:S(2)}) collective-permute-start(bf16[384,256]{1,0:T(8,128)(2,1)} %get-tuple-element.29), channel_id=1, source_target_pairs={{0,2},{2,4},{4,6},{6,8},{8,10},{10,12},{12,14},{14,16},{16,18},{18... | collective-permute-start | bytes 589832 | tf_op jit(solution)/shard_map/ppermute | solution.py:410
  85.2 1.2 %slice_bitcast_fusion = bf16[1,32,96,128]{3,2,1,0:T(8,128)(2,1)S(1)} fusion(bf16[40,96,128]{2,1,0:T(8,128)(2,1)} %copy-done.1), kind=kLoop, calls=%fused_computation.6 | loop fusion | bytes 1572864 | tf_op jit(solution)/shard_map/stack | solution.py:407
  86.4 0.0 copy-done.2
  86.4 0.3 maximum_select_fusion
  86.7 1.8 %copy.46 = bf16[64,96,128]{2,0,1:T(8,128)(2,1)} copy(bf16[64,96,128]{2,1,0:T(8,128)(2,1)S(1)} %bitcast.22) | data formatting | bytes 3145728 | tf_op jit(solution)/shard_map/jit(_where)/select_n | solution.py:407
  88.4 0.0 collective-permute-done.8.right_in
  88.4 2.0 %collective-permute-done.7.left_in = bf16[384,256]{1,0:T(8,128)(2,1)S(1)} collective-permute-done((bf16[384,256]{1,0:T(8,128)(2,1)}, bf16[384,256]{1,0:T(8,128)(2,1)S(1)}, u32[]{:S(2)}, u32[]{:S(2)}) %collective-permute-start.7) | collective-permute-done | bytes 196640 | tf_op jit(solution)/shard_map/ppermute | solution.py:410
  90.4 0.0 copy-done.5
  90.4 0.7 copy-done.6
  91.1 14.5 %section_two.1 = (bf16[8,192,128]{2,1,0:T(8,128)(2,1)}, bf16[8,192,128]{2,1,0:T(8,128)(2,1)}) custom-call(bf16[14,384,128]{2,1,0:T(8,128)(2,1)} %get-tuple-element.28.whole, bf16[384,256]{1,0:T(8,128)(2,1)} %copy-done.6, bf16[384,256]{1,0:T(8,128)(2,1)} %copy-done.5, bf16[3552,384]{1,0:T(8,128)(2,1)} %turn_weights.1.taps_own.columns_own.packed_own, ...), custom_call_target="tpu_custom_call" | custom-call | flops 10000000000 | bytes 10000000 | tf_op jit(solution)/shard_map/section_two/pallas_call | solution.py:26
  105.6 8.6 %collective-permute-start.9 = (bf16[8,192,128]{2,1,0:T(8,128)(2,1)}, bf16[8,192,128]{2,1,0:T(8,128)(2,1)S(1)}, u32[]{:S(2)}, u32[]{:S(2)}) collective-permute-start(bf16[8,192,128]{2,1,0:T(8,128)(2,1)} %get-tuple-element.31), channel_id=1, source_target_pairs={{0,1},{1,0},{2,3},{3,2},{4,5},{5,4},{6,7},{7,6},{8,9},{9,8},{10,11... | collective-permute-start | bytes 1179656 | tf_op jit(solution)/shard_map/ppermute | solution.py:401
  114.2 1.2 %copy.40 = bf16[8,192,128]{1,2,0:T(8,128)(2,1)S(1)} copy(bf16[8,192,128]{2,1,0:T(8,128)(2,1)} %get-tuple-element.30) | data formatting | bytes 786432 | tf_op jit(solution)/shard_map/section_two/pallas_call | solution.py:26
  115.4 0.4 collective-permute-done.9
  115.8 0.2 copy.41
  116.0 0.3 fusion
  116.3 1.0 copy.42
  (9 shorter events, 0.0 us)
Async XLA Ops:
  2.5 4.6 %collective-permute-start = (bf16[35,96,128]{2,1,0:T(8,128)(2,1)S(1)}, bf16[35,96,128]{2,1,0:T(8,128)(2,1)}, u32[]{:S(2)}, u32[]{:S(2)}) collective-permute-start(bf16[35,96,128]{2,1,0:T(8,128)(2,1)S(1)} %bitcast.27), channel_id=1, source_target_pairs={{0,1},{1,0},{2,3},{3,2},{4,5},{5,4},{6,7},{7,6},{8,9},{9,8},{10,11... | collective-permute-start | bytes 2580488 | tf_op jit(solution)/shard_map/ppermute | solution.py:401
  3.2 4.1 %copy-start = (bf16[96,64,128]{2,1,0:T(8,128)(2,1)S(1)}, bf16[96,64,128]{2,1,0:T(8,128)(2,1)}, u32[]{:S(2)}) copy-start(bf16[96,64,128]{2,1,0:T(8,128)(2,1)} %param.23) | copy-start | bytes 4718596
  7.1 26.1 %collective-permute-start.4 = (bf16[3552,384]{1,0:T(8,128)(2,1)}, bf16[3552,384]{1,0:T(8,128)(2,1)}, u32[]{:S(2)}, u32[]{:S(2)}) collective-permute-start(bf16[3552,384]{1,0:T(8,128)(2,1)} %turn_weights.1.taps_own.columns_own.packed_own), channel_id=1, source_target_pairs={{0,1},{1,0},{2,3},{3,2},{4,5},{5,4},{6,7},{7,6},{8,9},{9,8},{10,11... | collective-permute-start | bytes 8183816 | tf_op jit(solution)/shard_map/ppermute | solution.py:401
  9.2 6.5 %collective-permute-start.1 = (bf16[3,192,128]{2,1,0:T(8,128)(2,1)S(1)}, bf16[3,192,128]{2,1,0:T(8,128)(2,1)S(1)}, u32[]{:S(2)}, u32[]{:S(2)}) collective-permute-start(bf16[3,192,128]{2,1,0:T(8,128)(2,1)S(1)} %pad_maximum_fusion), channel_id=1, source_target_pairs={{1,32},{33,64},{65,96},{97,128},{129,160},{161,192},{193,224},{32,... | collective-permute-start | bytes 442376 | tf_op jit(solution)/shard_map/ppermute | solution.py:404
  15.7 0.7 copy-start.4
  20.5 7.0 %collective-permute-start.3 = (bf16[192,256]{1,0:T(8,128)(2,1)}, bf16[192,256]{1,0:T(8,128)(2,1)S(1)}, u32[]{:S(2)}, u32[]{:S(2)}) collective-permute-start(bf16[192,256]{1,0:T(8,128)(2,1)} %get-tuple-element.20), channel_id=1, source_target_pairs={{2,0},{4,2},{6,4},{8,6},{10,8},{12,10},{14,12},{16,14},{18,16},{20... | collective-permute-start | bytes 294920 | tf_op jit(solution)/shard_map/ppermute | solution.py:410
  25.6 7.7 %collective-permute-start.2 = (bf16[192,256]{1,0:T(8,128)(2,1)}, bf16[192,256]{1,0:T(8,128)(2,1)S(1)}, u32[]{:S(2)}, u32[]{:S(2)}) collective-permute-start(bf16[192,256]{1,0:T(8,128)(2,1)} %get-tuple-element.20), channel_id=1, source_target_pairs={{0,2},{2,4},{4,6},{6,8},{8,10},{10,12},{12,14},{14,16},{16,18},{18... | collective-permute-start | bytes 294920 | tf_op jit(solution)/shard_map/ppermute | solution.py:410
  27.5 5.8 %copy-start.7 = (bf16[192,256]{1,0:T(8,128)(2,1)}, bf16[192,256]{1,0:T(8,128)(2,1)S(1)}, u32[]{:S(2)}) copy-start(bf16[192,256]{1,0:T(8,128)(2,1)S(1)} %collective-permute-done.3.right_in) | copy-start | bytes 294916
  33.3 0.6 copy-start.8
  57.0 16.8 %collective-permute-start.5 = (bf16[40,96,128]{2,1,0:T(8,128)(2,1)}, bf16[40,96,128]{2,1,0:T(8,128)(2,1)S(1)}, u32[]{:S(2)}, u32[]{:S(2)}) collective-permute-start(bf16[40,96,128]{2,1,0:T(8,128)(2,1)} %get-tuple-element.23), channel_id=1, source_target_pairs={{0,1},{1,0},{2,3},{3,2},{4,5},{5,4},{6,7},{7,6},{8,9},{9,8},{10,11... | collective-permute-start | bytes 2949128 | tf_op jit(solution)/shard_map/ppermute | solution.py:401
  66.6 7.2 %collective-permute-start.6 = (bf16[8,96,128]{2,1,0:T(8,128)(2,1)}, bf16[8,96,128]{2,1,0:T(8,128)(2,1)S(1)}, u32[]{:S(2)}, u32[]{:S(2)}) collective-permute-start(bf16[8,96,128]{2,1,0:T(8,128)(2,1)} %get-tuple-element.24), channel_id=1, source_target_pairs={{1,32},{33,64},{65,96},{97,128},{129,160},{161,192},{193,224},{32,... | collective-permute-start | bytes 589832 | tf_op jit(solution)/shard_map/ppermute | solution.py:404
  73.8 0.7 copy-start.3
  73.8 1.0 copy-start.1
  74.8 11.6 %copy-start.2 = (bf16[32,96,128]{2,1,0:T(8,128)(2,1)S(1)}, bf16[32,96,128]{2,1,0:T(8,128)(2,1)}, u32[]{:S(2)}) copy-start(bf16[32,96,128]{2,1,0:T(8,128)(2,1)} %get-tuple-element.26) | copy-start | bytes 2359300
  79.8 8.7 %collective-permute-start.8 = (bf16[384,256]{1,0:T(8,128)(2,1)}, bf16[384,256]{1,0:T(8,128)(2,1)S(1)}, u32[]{:S(2)}, u32[]{:S(2)}) collective-permute-start(bf16[384,256]{1,0:T(8,128)(2,1)} %get-tuple-element.29), channel_id=1, source_target_pairs={{2,0},{4,2},{6,4},{8,6},{10,8},{12,10},{14,12},{16,14},{18,16},{20... | collective-permute-start | bytes 589832 | tf_op jit(solution)/shard_map/ppermute | solution.py:410
  81.7 8.7 %collective-permute-start.7 = (bf16[384,256]{1,0:T(8,128)(2,1)}, bf16[384,256]{1,0:T(8,128)(2,1)S(1)}, u32[]{:S(2)}, u32[]{:S(2)}) collective-permute-start(bf16[384,256]{1,0:T(8,128)(2,1)} %get-tuple-element.29), channel_id=1, source_target_pairs={{0,2},{2,4},{4,6},{6,8},{8,10},{10,12},{12,14},{14,16},{16,18},{18... | collective-permute-start | bytes 589832 | tf_op jit(solution)/shard_map/ppermute | solution.py:410
  88.4 2.0 %copy-start.5 = (bf16[384,256]{1,0:T(8,128)(2,1)}, bf16[384,256]{1,0:T(8,128)(2,1)S(1)}, u32[]{:S(2)}) copy-start(bf16[384,256]{1,0:T(8,128)(2,1)S(1)} %collective-permute-done.8.right_in) | copy-start | bytes 589828
  90.4 0.7 copy-start.6
  105.6 10.2 %collective-permute-start.9 = (bf16[8,192,128]{2,1,0:T(8,128)(2,1)}, bf16[8,192,128]{2,1,0:T(8,128)(2,1)S(1)}, u32[]{:S(2)}, u32[]{:S(2)}) collective-permute-start(bf16[8,192,128]{2,1,0:T(8,128)(2,1)} %get-tuple-element.31), channel_id=1, source_target_pairs={{0,1},{1,0},{2,3},{3,2},{4,5},{5,4},{6,7},{7,6},{8,9},{9,8},{10,11... | collective-permute-start | bytes 1179656 | tf_op jit(solution)/shard_map/ppermute | solution.py:401
